TPU v7x, 256 devices: a whole 4x4x8 slice. The times are simulated.
256 devices in a mesh: slot: 32 (over x, z), tp: 8 (over y, core).
Axes of the slice: x: 4, y: 4, z: 8, core: 2. Of those that a mesh axis runs over, the one named last changes fastest.
Arguments:
- queries: bfloat16 [8192, 6144], P('slot', 'tp'), may hold values from -150 to 150
- k_new: bfloat16 [8192, 6144], P('slot', 'tp'), may hold values from -7 to 7
- v_new: bfloat16 [8192, 6144], P('slot', 'tp'), may hold values from -6 to 6
- k_clean: bfloat16 [8192, 6144], P('slot', 'tp'), may hold values from -6 to 6
- v_clean: bfloat16 [8192, 6144], P('slot', 'tp'), may hold values from -6 to 6
- lists: int32 [32, 62], replicated, may hold values from 0 to 495, as said below
- counts: int32 [32], replicated, may hold values from 0 to 62, as said below
- resid: bfloat16 [8192, 6144], P('slot', 'tp'), may hold values from -1.5 to 1.5
- w_out: bfloat16 [6144, 6144], P('tp', 'slot'), may hold values from -0.29882812 to 0.29882812
Outputs:
- layer_out: bfloat16 [8192, 6144], P('slot', 'tp')
Inputs may be any that keep to these rules, and one draw needn't show every extreme that they name: Row c lists only blocks of groups before c, no block twice, at most 2 blocks of one group and exactly 2 of group c-1, in group order; entries from counts[c] on are 0 and unused. counts[c] lies between c and 2 * c; the last group reads exactly 2 blocks of every earlier group.
All inputs are finite; a program needn't handle non-finite values.
Results may differ from a plain program's by a relative error of at most 0.02.
Values may be sent and summed in bfloat16 or wider, within the bound.
A program may use at most 192 MiB of HBM per device.

v0:
```python
import math

import jax
import jax.numpy as jnp
from jax import lax
from jax.sharding import PartitionSpec as P

HEAD_DIM = 128
BLK = 16


def per_device(queries, k_new, v_new, k_clean, v_clean, lists, counts, resid, w_out):
    rows = queries.shape[0]
    heads = queries.shape[1] // HEAD_DIM
    scale = 1.0 / math.sqrt(HEAD_DIM)
    q_three = queries.reshape(rows, heads, HEAD_DIM)

    def scores(keys):
        k_three = keys.reshape(keys.shape[0], heads, HEAD_DIM)
        return (
            jnp.einsum("qhd,khd->hqk", q_three, k_three, preferred_element_type=jnp.float32) * scale
        )

    def weigh(ex, vals):
        v_three = vals.reshape(vals.shape[0], heads, HEAD_DIM)
        return jnp.einsum(
            "hqk,khd->hqd", ex.astype(jnp.bfloat16), v_three, preferred_element_type=jnp.float32
        )

    own = scores(k_new)
    top = jnp.max(own, -1)
    ex = jnp.exp(own - top[..., None])
    state = (top, jnp.sum(ex, -1), weigh(ex, v_new))
    maxr = lists.shape[1]
    me = lax.axis_index("slot")
    mylist = lax.dynamic_slice_in_dim(lists, me, 1, 0)[0]
    mycount = lax.dynamic_slice_in_dim(counts, me, 1, 0)[0]
    live = jnp.arange(maxr, dtype=jnp.int32) < mycount
    k_piece = lax.all_gather(k_clean, "slot", axis=0, tiled=True)
    v_piece = lax.all_gather(v_clean, "slot", axis=0, tiled=True)
    block_ids = jnp.arange(k_piece.shape[0], dtype=jnp.int32) // BLK
    allowed = jnp.any((block_ids[:, None] == mylist[None, :]) & live[None, :], 1)
    top, total, acc = state
    sc = jnp.where(allowed[None, None, :], scores(k_piece), -jnp.inf)
    top_new = jnp.maximum(top, jnp.max(sc, -1))
    fade = jnp.exp(top - top_new)
    ex = jnp.exp(sc - top_new[..., None])
    state = (top_new, total * fade + jnp.sum(ex, -1), acc * fade[..., None] + weigh(ex, v_piece))
    top, total, acc = state
    attn = (
        jnp.transpose(acc / total[..., None], (1, 0, 2))
        .reshape(rows, heads * HEAD_DIM)
        .astype(jnp.bfloat16)
    )
    terms = jnp.dot(
        attn, lax.all_gather(w_out, "slot", axis=1, tiled=True), preferred_element_type=jnp.float32
    )
    summed = lax.psum_scatter(
        terms.astype(jnp.bfloat16), "tp", scatter_dimension=1, tiled=True
    ).astype(jnp.float32)
    return (resid.astype(jnp.float32) + summed).astype(jnp.bfloat16)


def solution(mesh):
    in_specs = (
        P("slot", "tp"),
        P("slot", "tp"),
        P("slot", "tp"),
        P("slot", "tp"),
        P("slot", "tp"),
        P(),
        P(),
        P("slot", "tp"),
        P("tp", "slot"),
    )
    out_specs = P("slot", "tp")
    return jax.shard_map(
        per_device, mesh=mesh, in_specs=in_specs, out_specs=out_specs, check_vma=False
    )
```

profile of v0, /device:TPU:1, one launch (start us, length us, event | category | flops | bytes accessed | tf_op | source)
XLA Modules:
  0.0 415.7 jit_solution(12650717890673864106)
XLA Ops:
  6.5 0.0 copy-start
  6.5 0.0 all-gather.4.cloned.1.call-start
  6.5 1.9 copy.32
  8.5 0.0 all-gather.4.cloned.1.call-update
  8.5 0.0 all-gather.6.cloned.1.call-start
  8.5 0.7 all-gather.6.cloned.1.call-update
  9.2 0.0 all-gather.8.cloned.1.call-start
  9.3 0.7 all-gather.8.cloned.1.call-update
  10.0 0.0 reduce-scatter.2.cloned.1.call-start
  10.0 1.2 copy.26
  11.2 1.2 copy.27
  12.4 1.2 copy.30
  13.5 1.2 dynamic_slice.7
  14.8 0.0 copy-done
  14.8 0.6 iota_compare_fusion
  15.4 0.4 and_reduce_fusion
  15.8 0.4 fusion.24
  16.2 0.2 fusion.6
  16.5 121.8 %all-gather.4.cloned.1.call-done = bf16[8192,768]{0,1:T(8,128)(2,1)} async-done(((bf16[256,768]{0,1:T(8,128)(2,1)}), bf16[8192,768]{0,1:T(8,128)(2,1)}) %all-gather.4.cloned.1.call-update) | async-done | bytes 12582928 | tf_op jit(solution)/shard_map/all_gather | solution.py:39
  138.3 23.6 %fusion = (f32[6,256]{1,0:T(8,128)S(1)}, f32[6,256,8192]{2,1,0:T(8,128)}) fusion(pred[8192]{0:T(1024)(128)(4,1)S(1)} %and_reduce_fusion, bf16[256,6,128]{0,2,1:T(8,128)(2,1)S(1)} %bitcast.44, bf16[8192,6,128]{0,2,1:T(8,128)(2,1)} %bitcast.42), kind=kOutput, calls=%fused_computation.2 | convolution fusion | flops 3258972672 | bytes 63322112 | tf_op jit(solution)/shard_map/qhd,khd->hqk/dot_general | solution.py:21
  161.9 97.6 %all-gather.6.cloned.1.call-done = bf16[8192,768]{1,0:T(8,128)(2,1)} async-done(((bf16[256,768]{1,0:T(8,128)(2,1)}), bf16[8192,768]{1,0:T(8,128)(2,1)}) %all-gather.6.cloned.1.call-update) | async-done | bytes 12582928 | tf_op jit(solution)/shard_map/all_gather | solution.py:40
  259.5 15.8 %copy.35 = bf16[8192,768]{0,1:T(8,128)(2,1)} copy(bf16[8192,768]{1,0:T(8,128)(2,1)} %all-gather.6.cloned.1.call-done) | data formatting | bytes 25165824 | tf_op jit(solution)/shard_map/all_gather | solution.py:40
  275.3 22.1 %fusion.1 = f32[6,256]{1,0:T(8,128)S(1)} fusion(f32[6,256,8192]{2,1,0:T(8,128)} %get-tuple-element.10, f32[6,256]{1,0:T(8,128)S(1)} %max.18, pred[8192]{0:T(1024)(128)(4,1)S(1)} %and_reduce_fusion), kind=kLoop, calls=%fused_computation.3 | loop fusion | flops 50330112 | bytes 50352128 | tf_op jit(solution)/shard_map/reduce_sum | solution.py:48
  297.4 24.1 %fusion.11 = f32[256,6,128]{0,2,1:T(8,128)S(1)} fusion(bf16[8192,6,128]{0,2,1:T(8,128)(2,1)} %bitcast.41, f32[6,256,8192]{2,1,0:T(8,128)} %get-tuple-element.10, f32[6,256]{1,0:T(8,128)S(1)} %max.18, pred[8192]{0:T(1024)(128)(4,1)S(1)} %and_reduce_fusion), kind=kOutput, calls=%fused_computation.17 | convolution fusion | flops 3271557120 | bytes 63715328 | tf_op jit(solution)/shard_map/hqk,khd->hqd/dot_general | solution.py:26
  321.5 0.4 fusion.14
  321.9 40.8 %all-gather.8.cloned.1.call-done = bf16[768,6144]{0,1:T(8,128)(2,1)} async-done(((bf16[768,192]{0,1:T(8,128)(2,1)}), bf16[768,6144]{0,1:T(8,128)(2,1)}) %all-gather.8.cloned.1.call-update) | async-done | bytes 9437200 | tf_op jit(solution)/shard_map/all_gather | solution.py:56
  362.7 0.0 copy-start.1
  362.7 0.0 copy-start.2
  362.7 11.4 %convolution_convert_fusion = bf16[256,6144]{1,0:T(8,128)(2,1)} fusion(bf16[256,768]{0,1:T(8,128)(2,1)S(1)} %bitcast.47, bf16[768,6144]{0,1:T(8,128)(2,1)} %all-gather.8.cloned.1.call-done), kind=kOutput, calls=%fused_computation.7 | convolution fusion | flops 2417491968 | bytes 12976128 | tf_op jit(solution)/shard_map/dot_general | solution.py:55
  374.0 0.0 reduce-scatter.2.cloned.1.call-update
  374.1 33.2 %reduce-scatter.2.cloned.1.call-done = bf16[256,768]{1,0:T(8,128)(2,1)} async-done(((bf16[256,6144]{1,0:T(8,128)(2,1)}), bf16[256,768]{1,0:T(8,128)(2,1)}) %reduce-scatter.2.cloned.1.call-update) | async-done | bytes 393232 | tf_op jit(solution)/shard_map/reduce_scatter | solution.py:58
  407.3 0.0 copy-done.2
  407.3 1.8 add_convert_fusion
  409.1 0.0 copy-done.1
  (4 shorter events, 0.0 us)
Async XLA Ops:
  6.5 8.2 %copy-start = (s32[32,62]{1,0:T(8,128)S(1)}, s32[32,62]{1,0:T(8,128)}, u32[]{:S(2)}) copy-start(s32[32,62]{1,0:T(8,128)} %param.14) | copy-start | bytes 23812
  6.5 131.8 %all-gather.4.cloned.1.call-start = ((), (), s32[]{:S(2)}) async-start(), calls=%async_computation.1 | async-start | bytes 12976128 | tf_op jit(solution)/shard_map/all_gather | solution.py:39
  8.5 251.0 %all-gather.6.cloned.1.call-start = ((), (), s32[]{:S(2)}) async-start(), calls=%async_computation.2 | async-start | bytes 12976128 | tf_op jit(solution)/shard_map/all_gather | solution.py:40
  9.2 353.4 %all-gather.8.cloned.1.call-start = ((), (), s32[]{:S(2)}) async-start(), calls=%async_computation.3 | async-start | bytes 9732096 | tf_op jit(solution)/shard_map/all_gather | solution.py:56
  10.0 397.3 %reduce-scatter.2.cloned.1.call-start = ((), (), s32[]{:S(2)}) async-start(), calls=%async_computation.4 | async-start | bytes 3538944 | tf_op jit(solution)/shard_map/reduce_scatter | solution.py:58
  362.7 46.4 %copy-start.1 = (s32[32,62]{1,0:T(8,128)S(1)}, s32[32,62]{1,0:T(8,128)}, u32[]{:S(2)}) copy-start(s32[32,62]{1,0:T(8,128)} %param.14) | copy-start | bytes 23812
  362.7 44.6 %copy-start.2 = (bf16[256,768]{1,0:T(8,128)(2,1)S(1)}, bf16[256,768]{1,0:T(8,128)(2,1)}, u32[]{:S(2)}) copy-start(bf16[256,768]{1,0:T(8,128)(2,1)} %param.16) | copy-start | bytes 1179652
Sparse Core Ops, SparseCore 0:
  9.8 128.4 all-gather.3
  140.9 118.5 all-gather.5
  262.1 100.5 all-gather.7
  374.2 33.0 reduce-scatter.1
where the time goes:
time: 418 us; the launch traced here: 416 us
  waiting for transfers between devices  295 us (71%)
  matrix products  59.9 us (14%)
  other arithmetic  25.1 us (6%)
  local copies, waits for them, and re-layouts  22.5 us (5%)
  between operations  13.2 us (3%)
    all_gather x1, waiting for transfers between devices, per_device(): k_piece = lax.all_gather(k_clean, 'slot', axis=0, tiled=True)  122 us
    all_gather x1, waiting for transfers between devices, per_device(): v_piece = lax.all_gather(v_clean, 'slot', axis=0, tiled=True)  97.6 us
    all_gather x1, waiting for transfers between devices, per_device(): lax.all_gather(w_out, 'slot', axis=1, tiled=True)  40.8 us
    reduce_scatter x1, waiting for transfers between devices, per_device(): lax.psum_scatter(terms.astype(jnp.bfloat16), 'tp', scatter_dimension=1, t...  33.2 us
    dot_general x2, matrix products, weigh(): jnp.einsum('hqk,khd->hqd', ex.astype(jnp.bfloat16), v_three, preferred_el...  24.5 us
    dot_general x2, matrix products, scores(): jnp.einsum('qhd,khd->hqk', q_three, k_three, preferred_element_type=jnp.f...  24 us
    reduce_sum x1, other arithmetic, per_device(): jnp.sum(ex, -1)  22.1 us
    all_gather x1, local copies, waits for them, and re-layouts, per_device(): v_piece = lax.all_gather(v_clean, 'slot', axis=0, tiled=True)  15.8 us
  transfers between devices with their start and end apart: 4, of which 4 were waited for; matrix products, arithmetic and copies ran while one was open for 22% of the time, Pallas kernels for 0%

commit v1 on v0

v1 whole, which is shorter than its diff:
```python
import math

import jax
import jax.numpy as jnp
from jax import lax
from jax.experimental import pallas as pl
from jax.experimental.pallas import tpu as pltpu
from jax.sharding import PartitionSpec as P

HD = 128
BLK = 16
NX, NZ, NY = 4, 8, 4
RING = (1, 7, 2, 6, 3, 5, 4)
MESH = pl.DeviceIdType.MESH
BF = jnp.bfloat16
F32 = jnp.float32
NEG = -1e30
NT = (((1,), (1,)), ((), ()))
VM = pltpu.VMEM
DMA = pltpu.SemaphoreType.DMA


def remote(src, dst, ssem, rsem, **where):
    return pltpu.make_async_remote_copy(
        src_ref=src, dst_ref=dst, send_sem=ssem, recv_sem=rsem, device_id=where, device_id_type=MESH
    )


def loop(lo, hi, body):
    def step(i, c):
        body(i)
        return c

    lax.fori_loop(lo, hi, step, 0)


def attention_kernel(
    q, kn, vn, kc, vc, wt, lists, counts,
    attn, wall,
    sk, sv, kb, vb, rk, rv, wz, hot, seen, mx, tot, acc,
    k1s, k1r, k2s, k2r, v1s, v1r, v2s, v2r, os, orr, w1s, w1r, wps, wpr, wms, wmr, wcs, wcr,
):
    me = lax.axis_index("slot")
    tp = lax.axis_index("tp")
    x, z, core = me // NZ, me % NZ, tp % 2
    sib = tp + 1 - 2 * core
    heads = q.shape[1] // HD
    c2 = math.log2(math.e) / math.sqrt(HD)

    def at(ax, az):
        return ax * NZ + az

    barrier = pltpu.get_barrier_semaphore()
    for d in range(1, NX):
        pl.semaphore_signal(barrier, inc=1, device_id={"slot": at((x + d) % NX, z)}, device_id_type=MESH)
    for d in range(1, NZ):
        pl.semaphore_signal(barrier, inc=1, device_id={"slot": at(x, (z + d) % NZ)}, device_id_type=MESH)
    pl.semaphore_signal(barrier, inc=1, device_id={"tp": sib}, device_id_type=MESH)

    lst = lists[...]
    live = lax.broadcasted_iota(jnp.int32, lst.shape, 1) < counts[...]
    mine = live & (lst // BLK == me)
    within = lst % BLK
    lo = jnp.min(jnp.where(mine, within, 1000), 1, keepdims=True)
    hi = jnp.max(jnp.where(mine, within, -1), 1, keepdims=True)
    hi = jnp.where(hi == lo, 1000, hi)
    lo = jnp.where(lo < 0, 1000, lo)
    hi = jnp.where(hi < 0, 1000, hi)
    readers = lst.shape[0]
    lo_b = jnp.broadcast_to(lo.astype(F32), (readers, 256)).astype(BF)
    hi_b = jnp.broadcast_to(hi.astype(F32), (readers, 256)).astype(BF)

    row = lists[pl.ds(me, 1), :]
    n_live = counts[pl.ds(me, 1), :]
    row_live = lax.broadcasted_iota(jnp.int32, row.shape, 1) < n_live
    owner = lax.broadcasted_iota(jnp.int32, lst.shape, 0)
    n_of = jnp.sum(jnp.where((row // BLK == owner) & row_live, 1, 0), 1, keepdims=True)
    for x1 in range(NX):
        key = lax.broadcasted_iota(jnp.int32, (readers, 256), 1)
        own_of = lax.broadcasted_iota(jnp.int32, (readers, 256), 0)
        cnt = jnp.sum(jnp.where(own_of == x1 * NZ + key // 32, n_of, 0), 0, keepdims=True)
        part = (lax.broadcasted_iota(jnp.int32, (1, 256), 1) // BLK) % 2
        seen[x1] = jnp.broadcast_to(jnp.where(cnt > part, 1.0, 0.0), (8, 256))

    def pack(x2):
        r = lax.broadcasted_iota(jnp.int32, (256, readers), 0) // 32 + x2 * NZ
        pick = (r == lax.broadcasted_iota(jnp.int32, (256, readers), 1)).astype(F32).astype(BF)
        first = jnp.dot(pick, lo_b, preferred_element_type=F32)
        second = jnp.dot(pick, hi_b, preferred_element_type=F32)
        rows = lax.broadcasted_iota(jnp.int32, (256, 256), 0)
        cols = lax.broadcasted_iota(jnp.int32, (256, 256), 1)
        blk = jnp.where((rows // BLK) % 2 == 0, first, second)
        want = blk * BLK + (rows % BLK).astype(F32)
        hot[...] = jnp.where(want == cols.astype(F32), 1.0, 0.0).astype(BF)
        sk[x2] = jnp.dot(hot[...], kc[...], preferred_element_type=F32).astype(BF).reshape(NZ, 32, kc.shape[1])
        sv[x2] = jnp.dot(hot[...], vc[...], preferred_element_type=F32).astype(BF).reshape(NZ, 32, kc.shape[1])

    loop(x, NX, pack)
    wz[z, x] = wt[x]
    pl.semaphore_wait(barrier, NX - 1 + NZ - 1 + 1)

    for d in (1, 3, 2):
        x2 = (x + d) % NX
        remote(wt.at[x2], wz.at[z, x], w1s.at[x2], w1r.at[x], slot=at(x2, z)).start()
    for d in RING + (0,):
        z2 = (z + d) % NZ
        if d:
            @pl.when(z2 > z)
            def _():
                remote(sk.at[x, z2], rk.at[x, z], os.at[0, z2], orr.at[0, z], slot=at(x, z2)).start()
                remote(sv.at[x, z2], rv.at[x, z], os.at[1, z2], orr.at[1, z], slot=at(x, z2)).start()

        def out(x2):
            if d:
                remote(sk.at[x2, z2], kb.at[x, z2], k1s.at[x2, z2], k1r.at[x, z2], slot=at(x2, z)).start()
                remote(sv.at[x2, z2], vb.at[x2, z], v1s.at[x2, z2], v1r.at[x2, z], slot=at(x, z2)).start()
            else:
                remote(sk.at[x2, z], rk.at[x, z], k2s.at[x2, z], k2r.at[x, z], slot=at(x2, z)).start()
                remote(sv.at[x2, z], rv.at[x, z], v2s.at[x2, z], v2r.at[x, z], slot=at(x2, z)).start()

        loop(x + 1, NX, out)

    def blank(z1):
        rk[x, z1] = jnp.zeros(rk.shape[2:], BF)
        rv[x, z1] = jnp.zeros(rv.shape[2:], BF)

    loop(z, NZ, blank)

    for h in range(heads):
        cols = slice(h * HD, (h + 1) * HD)
        s = lax.dot_general(q[:, cols], kn[:, cols], NT, preferred_element_type=F32)
        top = jnp.max(s, 1, keepdims=True)
        p = jnp.exp2((s - top) * c2)
        mx[h] = jnp.broadcast_to(top, (256, HD))
        tot[h] = jnp.broadcast_to(jnp.sum(p, 1, keepdims=True), (256, HD))
        acc[:, cols] = jnp.dot(p.astype(BF), vn[:, cols], preferred_element_type=F32)

    def ring_step(k):
        zp, zm = (z + 1) % NZ, (z + NZ - 1) % NZ
        a, b = (z + NZ - k + 1) % NZ, (z + k - 1) % NZ
        if k > 1:
            remote(wz.at[a], wz.at[a], wps.at[k - 2], wpr.at[k - 2], slot=at(x, zp)).wait_recv()
            remote(wz.at[b], wz.at[b], wms.at[k - 2], wmr.at[k - 2], slot=at(x, zm)).wait_recv()
        if k < 4:
            remote(wz.at[a], wz.at[a], wps.at[k - 1], wpr.at[k - 1], slot=at(x, zp)).start()
            remote(wz.at[b], wz.at[b], wms.at[k - 1], wmr.at[k - 1], slot=at(x, zm)).start()
        else:
            remote(wz.at[a, pl.ds(0, 2)], wz.at[a, pl.ds(0, 2)], wps.at[3], wpr.at[3], slot=at(x, zp)).start()
            remote(wz.at[b, pl.ds(2, 2)], wz.at[b, pl.ds(2, 2)], wms.at[3], wmr.at[3], slot=at(x, zm)).start()

    for d in (1, 3, 2):
        x1 = (x + d) % NX
        remote(wt.at[x], wz.at[z, x1], w1s.at[x1], w1r.at[x1], slot=at(x1, z)).wait_recv()
    ring_step(1)

    for i, d in enumerate(RING):
        z2 = (z + d) % NZ

        def fwd_k(x1):
            remote(kb.at[x1, z2], kb.at[x1, z2], k1s.at[x, z2], k1r.at[x1, z2], slot=me).wait_recv()
            remote(kb.at[x1, z2], rk.at[x1, z], k2s.at[x1, z2], k2r.at[x1, z], slot=at(x, z2)).start()

        def fwd_v(x2):
            remote(vb.at[x2, z2], vb.at[x2, z2], v1s.at[x, z2], v1r.at[x2, z2], slot=me).wait_recv()
            remote(vb.at[x2, z2], rv.at[x, z2], v2s.at[x2, z2], v2r.at[x, z2], slot=at(x2, z)).start()

        loop(x + 1, NX, fwd_v)
        loop(0, x, fwd_k)
        if i == 3:
            ring_step(2)
    ring_step(3)

    def chunk(x1):
        ok = seen[x1][0:1, :] > 0.5
        for h in range(heads):
            cols = slice(h * HD, (h + 1) * HD)
            keys = rk[x1, :, :, cols].reshape(256, HD)
            vals = rv[x1, :, :, cols].reshape(256, HD)
            s = lax.dot_general(q[:, cols], keys, NT, preferred_element_type=F32)
            s = jnp.where(ok, s, NEG)
            old = mx[h][:, :1]
            top = jnp.maximum(old, jnp.max(s, 1, keepdims=True))
            fade = jnp.exp2((old - top) * c2)
            p = jnp.exp2((s - top) * c2)
            mx[h] = jnp.broadcast_to(top, (256, HD))
            tot[h] = tot[h] * fade + jnp.sum(p, 1, keepdims=True)
            acc[:, cols] = acc[:, cols] * fade + jnp.dot(p.astype(BF), vals, preferred_element_type=F32)

    def own_row(z1):
        remote(sk.at[x, z1], rk.at[x, z1], os.at[0, z1], orr.at[0, z1], slot=me).wait_recv()
        remote(sv.at[x, z1], rv.at[x, z1], os.at[1, z1], orr.at[1, z1], slot=me).wait_recv()

    loop(0, z, own_row)
    chunk(x)
    ring_step(4)

    def earlier(i):
        x1 = x - 1 - i
        for z1 in range(NZ):
            remote(sk.at[x1, z1], rk.at[x1, z1], k2s.at[x1, z1], k2r.at[x1, z1], slot=me).wait_recv()
            remote(sv.at[x1, z1], rv.at[x1, z1], v2s.at[x1, z1], v2r.at[x1, z1], slot=me).wait_recv()
        chunk(x1)

    loop(0, x, earlier)
    for h in range(heads):
        cols = slice(h * HD, (h + 1) * HD)
        attn[:, cols] = (acc[:, cols] / tot[h]).astype(BF)

    far = (z + 4) % NZ
    remote(wz.at[far, pl.ds(0, 2)], wz.at[far, pl.ds(0, 2)], wps.at[3], wpr.at[3], slot=me).wait_recv()
    remote(wz.at[far, pl.ds(2, 2)], wz.at[far, pl.ds(2, 2)], wms.at[3], wmr.at[3], slot=me).wait_recv()
    other = (1 - core) * 4
    swap = remote(wz.at[pl.ds(other, 4)], wall.at[core], wcs, wcr, tp=sib)
    swap.start()
    wall[core] = wz[pl.ds(core * 4, 4)]

    for d in (1, 3, 2):
        x2 = (x + d) % NX
        remote(wt.at[x2], wz.at[z, x], w1s.at[x2], w1r.at[x], slot=at(x2, z)).wait_send()
    for k in range(3):
        remote(wz.at[z], wz.at[z], wps.at[k], wpr.at[k], slot=me).wait_send()
        remote(wz.at[z], wz.at[z], wms.at[k], wmr.at[k], slot=me).wait_send()
    remote(wz.at[z, pl.ds(0, 2)], wz.at[z, pl.ds(0, 2)], wps.at[3], wpr.at[3], slot=me).wait_send()
    remote(wz.at[z, pl.ds(2, 2)], wz.at[z, pl.ds(2, 2)], wms.at[3], wmr.at[3], slot=me).wait_send()
    for d in RING + (0,):
        z2 = (z + d) % NZ
        if d:
            @pl.when(z2 > z)
            def _():
                remote(sk.at[x, z2], rk.at[x, z], os.at[0, z2], orr.at[0, z], slot=me).wait_send()
                remote(sv.at[x, z2], rv.at[x, z], os.at[1, z2], orr.at[1, z], slot=me).wait_send()

        def sent(x2):
            if d:
                remote(sk.at[x2, z2], kb.at[x, z2], k1s.at[x2, z2], k1r.at[x, z2], slot=me).wait_send()
                remote(sv.at[x2, z2], vb.at[x2, z], v1s.at[x2, z2], v1r.at[x2, z], slot=me).wait_send()
                remote(vb.at[x2, z2], rv.at[x, z2], v2s.at[x2, z2], v2r.at[x, z2], slot=me).wait_send()
            else:
                remote(sk.at[x2, z], rk.at[x, z], k2s.at[x2, z], k2r.at[x, z], slot=me).wait_send()
                remote(sv.at[x2, z], rv.at[x, z], v2s.at[x2, z], v2r.at[x, z], slot=me).wait_send()

        def passed(x1):
            remote(kb.at[x1, z2], rk.at[x1, z], k2s.at[x1, z2], k2r.at[x1, z], slot=me).wait_send()

        loop(x + 1, NX, sent)
        if d:
            loop(0, x, passed)
    swap.wait()


def projection_kernel(
    attn, w, resid,
    out,
    a, part, got, red, fin, flat,
    cs, cr, a1s, a1r, a2s, a2r, ys, yr, xs_, xr,
):
    me = lax.axis_index("slot")
    tp = lax.axis_index("tp")
    x, z, y, core = me // NZ, me % NZ, tp // 2, tp % 2
    sib = tp + 1 - 2 * core

    def at(ax):
        return ax * NZ + z

    left, right, across = (x + 3) % NX, (x + 1) % NX, (x + 2) % NX
    barrier = pltpu.get_barrier_semaphore()
    for d in range(1, NX):
        pl.semaphore_signal(barrier, inc=1, device_id={"slot": at((x + d) % NX)}, device_id_type=MESH)
        pl.semaphore_signal(barrier, inc=1, device_id={"tp": ((y + d) % NY) * 2 + core}, device_id_type=MESH)
    pl.semaphore_signal(barrier, inc=1, device_id={"tp": sib}, device_id_type=MESH)
    a[core, x] = attn[...]
    pl.semaphore_wait(barrier, NX - 1 + NY - 1 + 1)

    def to_sib(g):
        return remote(a.at[core, g], a.at[core, g], cs.at[g], cr.at[g], tp=sib)

    def from_sib(g):
        remote(a.at[1 - core, g], a.at[1 - core, g], cs.at[g], cr.at[g], tp=sib).wait_recv()

    to_sib(x).start()
    to_right = remote(a.at[core, x], a.at[core, x], a1s.at[0], a1r.at[0], slot=at(right))
    to_left = remote(a.at[core, x], a.at[core, x], a1s.at[1], a1r.at[1], slot=at(left))
    to_right.start()
    to_left.start()

    def share(g, d, peer):
        return remote(part.at[g, peer], got.at[g, y], ys.at[g, d - 1], yr.at[g, d - 1], tp=peer * 2 + core)

    def project(g):
        from_sib(g)
        for zs in range(4):
            o = lax.dot_general(w[0, zs].reshape(192, 768), a[0, g], NT, preferred_element_type=F32)
            o += lax.dot_general(w[1, zs].reshape(192, 768), a[1, g], NT, preferred_element_type=F32)
            for p in range(NY):
                part[g, p, zs * 48 : (zs + 1) * 48, :] = o[p * 48 : (p + 1) * 48].astype(BF)
        for d in (1, 3, 2):
            share(g, d, (y + d) % NY).start()

    def reduce(g):
        s = part[g, y].astype(F32)
        for d in (1, 3, 2):
            src = (y + NY - d) % NY
            remote(part.at[g, y], got.at[g, src], ys.at[g, d - 1], yr.at[g, d - 1], slot=me).wait_recv()
            s += got[g, src].astype(F32)
        return s.astype(BF)

    def home(d):
        g = (x + d) % NX
        return remote(red.at[g], fin.at[x], xs_.at[d - 1], xr.at[d - 1], slot=at(g))

    project(x)
    remote(a.at[core, left], a.at[core, left], a1s.at[0], a1r.at[0], slot=me).wait_recv()
    half_r = remote(a.at[core, left, pl.ds(0, 128)], a.at[core, left, pl.ds(0, 128)], a2s.at[0], a2r.at[0], slot=at(right))
    half_r.start()
    to_sib(left).start()
    remote(a.at[core, right], a.at[core, right], a1s.at[1], a1r.at[1], slot=me).wait_recv()
    half_l = remote(a.at[core, right, pl.ds(128, 128)], a.at[core, right, pl.ds(128, 128)], a2s.at[1], a2r.at[1], slot=at(left))
    half_l.start()
    to_sib(right).start()
    project(left)
    project(right)
    fin[x] = reduce(x)
    remote(a.at[core, across, pl.ds(0, 128)], a.at[core, across, pl.ds(0, 128)], a2s.at[0], a2r.at[0], slot=me).wait_recv()
    remote(a.at[core, across, pl.ds(128, 128)], a.at[core, across, pl.ds(128, 128)], a2s.at[1], a2r.at[1], slot=me).wait_recv()
    to_sib(across).start()
    project(across)
    for d in (3, 1, 2):
        g = (x + d) % NX
        red[g] = reduce(g)
        home(d).start()
    for d in (3, 1, 2):
        src = (x + NX - d) % NX
        remote(red.at[x], fin.at[src], xs_.at[d - 1], xr.at[d - 1], slot=me).wait_recv()
    for src in range(NX):
        for zs in range(4):
            flat[zs * 192 + src * 48 : zs * 192 + (src + 1) * 48, :] = fin[src, zs * 48 : (zs + 1) * 48, :]
    rows = lax.broadcasted_iota(jnp.int32, (256, 256), 0)
    cols = lax.broadcasted_iota(jnp.int32, (256, 256), 1)
    eye = jnp.where(rows == cols, 1.0, 0.0).astype(BF)
    summed = lax.dot_general(eye, flat[...], NT, preferred_element_type=F32)
    out[...] = (resid[...].astype(F32) + summed).astype(BF)

    for g in range(NX):
        to_sib(g).wait_send()
        for d in range(1, NY):
            share(g, d, (y + d) % NY).wait_send()
    to_right.wait_send()
    to_left.wait_send()
    half_r.wait_send()
    half_l.wait_send()
    for d in range(1, NX):
        home(d).wait_send()


def per_device(queries, k_new, v_new, k_clean, v_clean, lists, counts, resid, w_out):
    width = queries.shape[1]
    wt = w_out.T.reshape(NX, 48, width)
    vm = pl.BlockSpec(memory_space=VM)
    attn, wall = pl.pallas_call(
        attention_kernel,
        out_shape=(
            jax.ShapeDtypeStruct((256, width), BF),
            jax.ShapeDtypeStruct((2, 4, NX, 48, width), BF),
        ),
        in_specs=[vm] * 8,
        out_specs=(vm, vm),
        scratch_shapes=[
            VM((NX, NZ, 32, width), BF), VM((NX, NZ, 32, width), BF),
            VM((NX, NZ, 32, width), BF), VM((NX, NZ, 32, width), BF),
            VM((NX, NZ, 32, width), BF), VM((NX, NZ, 32, width), BF),
            VM((NZ, NX, 48, width), BF), VM((256, 256), BF), VM((NX, 8, 256), F32),
            VM((width // HD, 256, HD), F32), VM((width // HD, 256, HD), F32), VM((256, width), F32),
            DMA((NX, NZ)), DMA((NX, NZ)), DMA((NX, NZ)), DMA((NX, NZ)),
            DMA((NX, NZ)), DMA((NX, NZ)), DMA((NX, NZ)), DMA((NX, NZ)),
            DMA((2, NZ)), DMA((2, NZ)), DMA((NX,)), DMA((NX,)),
            DMA((4,)), DMA((4,)), DMA((4,)), DMA((4,)), DMA, DMA,
        ],
        compiler_params=pltpu.CompilerParams(
            collective_id=0, has_side_effects=True, vmem_limit_bytes=56 << 20
        ),
        name="attention",
    )(queries, k_new, v_new, k_clean, v_clean, wt, lists, counts.reshape(-1, 1))
    return pl.pallas_call(
        projection_kernel,
        out_shape=jax.ShapeDtypeStruct((256, width), BF),
        in_specs=[vm] * 3,
        out_specs=vm,
        scratch_shapes=[
            VM((2, NX, 256, width), BF), VM((NX, NY, 192, 256), BF), VM((NX, NY, 192, 256), BF),
            VM((NX, 192, 256), BF), VM((NX, 192, 256), BF), VM((width, 256), BF),
            DMA((NX,)), DMA((NX,)), DMA((2,)), DMA((2,)), DMA((2,)), DMA((2,)),
            DMA((NX, 3)), DMA((NX, 3)), DMA((3,)), DMA((3,)),
        ],
        compiler_params=pltpu.CompilerParams(
            collective_id=1, has_side_effects=True, vmem_limit_bytes=56 << 20
        ),
        name="projection",
    )(attn, wall, resid)


def solution(mesh):
    in_specs = (
        P("slot", "tp"),
        P("slot", "tp"),
        P("slot", "tp"),
        P("slot", "tp"),
        P("slot", "tp"),
        P(),
        P(),
        P("slot", "tp"),
        P("tp", "slot"),
    )
    out_specs = P("slot", "tp")
    return jax.shard_map(
        per_device, mesh=mesh, in_specs=in_specs, out_specs=out_specs, check_vma=False
    )
```

time: 418 us -> 132 us (0.32)
  waiting for transfers between devices: 295 us -> 0 us
  Pallas kernels: 0 us -> 129 us
  matrix products: 59.9 us -> 0 us
  other arithmetic: 25.1 us -> 0 us
  local copies, waits for them, and re-layouts: 22.5 us -> 3.11 us
  between operations: 13.2 us -> 0.02 us
    all_gather x3 -> x0, waiting for transfers between devices: 260 us -> none  [the longest x1 122 us: per_device(): k_piece = lax.all_gather(k_clean, 'slot', axis=0, tiled=True)]
    pallas_call x0 -> x2, Pallas kernels: none -> 129 us  [the longest x1 86.2 us: per_device(): pl.pallas_call(attention_kernel, out_shape=(jax.ShapeDtypeStruct((256, wi...]
    dot_general x5 -> x0, matrix products: 59.9 us -> none  [the longest x2 24.5 us: weigh(): jnp.einsum('hqk,khd->hqd', ex.astype(jnp.bfloat16), v_three, preferred_el...]
    reduce_scatter x1 -> x0, waiting for transfers between devices: 33.2 us -> none  [per_device(): lax.psum_scatter(terms.astype(jnp.bfloat16), 'tp', scatter_dimension=1, t...]
    reduce_sum x2 -> x0, other arithmetic: 22.3 us -> none  [the longest x1 22.1 us: per_device(): jnp.sum(ex, -1)]
    all_gather x1 -> x0, local copies, waits for them, and re-layouts: 15.8 us -> none  [per_device(): v_piece = lax.all_gather(v_clean, 'slot', axis=0, tiled=True)]
  transfers between devices with their start and end apart: 4 -> 0, of which waited for: 4 -> 0; matrix products, arithmetic and copies ran while one was open for 22% -> 0% of each run, Pallas kernels for 0% -> 0%
where the time goes in v1:
time: 132 us
  Pallas kernels  129 us (98%)
  local copies, waits for them, and re-layouts  3.11 us (2%)
    pallas_call x1, Pallas kernels, per_device(): pl.pallas_call(attention_kernel, out_shape=(jax.ShapeDtypeStruct((256, wi...  86.2 us
    pallas_call x1, Pallas kernels, per_device(): pl.pallas_call(projection_kernel, out_shape=jax.ShapeDtypeStruct((256, wi...  42.4 us

profile of v1, /device:TPU:1, one launch (start us, length us, event | category | flops | bytes accessed | tf_op | source)
XLA Modules:
  0.0 131.7 jit_solution(3784647136548423039)
XLA Ops:
  0.0 1.3 %copy.10.counts = s32[32,1]{1,0:T(8,128)} copy(s32[32,1]{0,1:T(1,128)} %bitcast.5) | data formatting | bytes 256 | tf_op jit(solution)/shard_map/reshape | solution.py:382
  1.3 86.2 %attention.1 = (bf16[256,768]{1,0:T(8,128)(2,1)}, bf16[2,4,4,48,768]{4,3,2,1,0:T(8,128)(2,1)}) custom-call(bf16[256,768]{1,0:T(8,128)(2,1)} %q.1, bf16[256,768]{1,0:T(8,128)(2,1)} %kn.1, bf16[256,768]{1,0:T(8,128)(2,1)} %vn.1, bf16[256,768]{1,0:T(8,128)(2,1)} %kc.1, bf16[256,768]{1,0:T(8,128)(2,1)} %vc.1, bf16[4,48,768]{2,1,0:T(8,128)(2,1)} %bitcast.4, ...), custom_call_target="tpu_custom_call" | custom-call | tf_op jit(solution)/shard_map/attention/pallas_call | solution.py:359
  87.6 42.4 %projection.1 = bf16[256,768]{1,0:T(8,128)(2,1)} custom-call(bf16[256,768]{1,0:T(8,128)(2,1)} %get-tuple-element.7.attn, bf16[2,4,4,48,768]{4,3,2,1,0:T(8,128)(2,1)} %get-tuple-element.8.w, bf16[256,768]{1,0:T(8,128)(2,1)} %resid.1), custom_call_target="tpu_custom_call" | custom-call | tf_op jit(solution)/shard_map/projection/pallas_call | solution.py:383
  129.9 1.8 %copy.12 = bf16[256,768]{1,0:T(8,128)(2,1)} copy(bf16[256,768]{1,0:T(8,128)(2,1)} %projection.1) | data formatting | bytes 786432

commit v2 on v0

v2 whole, which is shorter than its diff:
```python
import math

import jax
import jax.numpy as jnp
from jax import lax
from jax.experimental import pallas as pl
from jax.experimental.pallas import tpu as pltpu
from jax.sharding import PartitionSpec as P

HD = 128
BLK = 16
NX, NZ, NY = 4, 8, 4
RING = (1, 7, 2, 6, 3, 5, 4)
MESH = pl.DeviceIdType.MESH
BF = jnp.bfloat16
F32 = jnp.float32
NEG = -1e30
NT = (((1,), (1,)), ((), ()))
VM = pltpu.VMEM
DMA = pltpu.SemaphoreType.DMA


def remote(src, dst, ssem, rsem, **where):
    return pltpu.make_async_remote_copy(
        src_ref=src, dst_ref=dst, send_sem=ssem, recv_sem=rsem, device_id=where, device_id_type=MESH
    )


def loop(lo, hi, body):
    def step(i, c):
        body(i)
        return c

    lax.fori_loop(lo, hi, step, 0)


def layer_kernel(
    q, kn, vn, kc, vc, wt, lists, counts, resid,
    out,
    sk, sv, kb, vb, rk, rv, wz, ws, seen, mx, tot, acc, tab, tabs,
    a, part, got, red, fin, flat,
    ts, k1s, k1r, k2s, k2r, v1s, v1r, v2s, v2r, os, orr, w1s, w1r, wps, wpr, wms, wmr, wcs, wcr,
    cs, cr, a1s, a1r, a2s, a2r, ys, yr, hs, hr,
):
    me = lax.axis_index("slot")
    tp = lax.axis_index("tp")
    x, z, y, core = me // NZ, me % NZ, tp // 2, tp % 2
    sib = tp + 1 - 2 * core
    left, right, across = (x + 3) % NX, (x + 1) % NX, (x + 2) % NX
    heads = q.shape[1] // HD
    c2 = math.log2(math.e) / math.sqrt(HD)

    def at(ax, az):
        return ax * NZ + az

    def put(src, dst, ssem, rsem, **where):
        remote(src, dst, ssem, rsem, **where).start()

    def take(dst, rsem):
        remote(dst, dst, rsem, rsem, slot=me).wait_recv()

    def sent(src, ssem):
        remote(src, src, ssem, ssem, slot=me).wait_send()

    barrier = pltpu.get_barrier_semaphore()
    for d in range(1, NX):
        pl.semaphore_signal(barrier, inc=1, device_id={"slot": at((x + d) % NX, z)}, device_id_type=MESH)
    for d in range(1, NZ):
        pl.semaphore_signal(barrier, inc=1, device_id={"slot": at(x, (z + d) % NZ)}, device_id_type=MESH)
    for d in range(1, NY):
        pl.semaphore_signal(barrier, inc=1, device_id={"tp": ((y + d) % NY) * 2 + core}, device_id_type=MESH)
    pl.semaphore_signal(barrier, inc=1, device_id={"tp": sib}, device_id_type=MESH)

    lst = lists[...]
    readers = lst.shape[0]
    sub = lax.broadcasted_iota(jnp.int32, (readers, 128), 0)
    lane = lax.broadcasted_iota(jnp.int32, (readers, 128), 1)
    live_n = jnp.sum(jnp.where(sub[:, :readers] == lane[:, :readers], counts[...], 0), 1, keepdims=True)
    live = lax.broadcasted_iota(jnp.int32, lst.shape, 1) < live_n
    mine = live & (lst // BLK == me)
    within = lst % BLK
    lo = jnp.min(jnp.where(mine, within, BLK), 1, keepdims=True)
    hi = jnp.max(jnp.where(mine, within, 0), 1, keepdims=True)
    lo = jnp.where(lo < BLK, lo, 0)
    tab[0:1, :] = jnp.sum(jnp.where(sub == lane, lo, 0), 0, keepdims=True)
    tab[1:2, :] = jnp.sum(jnp.where(sub == lane, hi, 0), 0, keepdims=True)
    to_scalar = pltpu.make_async_copy(tab, tabs, ts)
    to_scalar.start()

    row = lists[pl.ds(me, 1), :]
    n_live = jnp.sum(jnp.where(lax.broadcasted_iota(jnp.int32, counts.shape, 1) == me, counts[...], 0), 1, keepdims=True)
    row_live = lax.broadcasted_iota(jnp.int32, row.shape, 1) < n_live
    owner = lax.broadcasted_iota(jnp.int32, lst.shape, 0)
    n_of = jnp.sum(jnp.where((row // BLK == owner) & row_live, 1, 0), 1, keepdims=True)
    for x1 in range(NX):
        key = lax.broadcasted_iota(jnp.int32, (readers, 256), 1)
        own_of = lax.broadcasted_iota(jnp.int32, (readers, 256), 0)
        cnt = jnp.sum(jnp.where(own_of == x1 * NZ + key // 32, n_of, 0), 0, keepdims=True)
        odd = (lax.broadcasted_iota(jnp.int32, (1, 256), 1) // BLK) % 2
        seen[x1] = jnp.broadcast_to(jnp.where(cnt > odd, 1.0, 0.0), (8, 256))
    to_scalar.wait()

    def pack(x2):
        for z2 in range(NZ):
            r = at(x2, z2)
            for half in range(2):
                blk = tabs[half, r]
                sk[x2, z2, half * BLK : (half + 1) * BLK, :] = kc[blk]
                sv[x2, z2, half * BLK : (half + 1) * BLK, :] = vc[blk]

    pack(x)
    pl.semaphore_wait(barrier, NX - 1 + NZ - 1 + NY - 1 + 1)

    for d in RING:
        z2 = (z + d) % NZ

        @pl.when(z2 > z)
        def _():
            put(sk.at[x, z2], rk.at[x, z], os.at[0, z2], orr.at[0, z], slot=at(x, z2))
            put(sv.at[x, z2], rv.at[x, z], os.at[1, z2], orr.at[1, z], slot=at(x, z2))

    def give(x2):
        pack(x2)
        for d in RING:
            z2 = (z + d) % NZ
            put(sv.at[x2, z2], vb.at[x2, z], v1s.at[x2, z2], v1r.at[x2, z], slot=at(x, z2))
            put(sk.at[x2, z2], kb.at[x, z2], k1s.at[x2, z2], k1r.at[x, z2], slot=at(x2, z))
        put(sk.at[x2, z], rk.at[x, z], k2s.at[x2, z], k2r.at[x, z], slot=at(x2, z))
        put(sv.at[x2, z], rv.at[x, z], v2s.at[x2, z], v2r.at[x, z], slot=at(x2, z))

    loop(x + 1, NX, give)
    for d in (1, 3, 2):
        x2 = (x + d) % NX
        put(wt.at[x2], wz.at[z, x], w1s.at[x2], w1r.at[x], slot=at(x2, z))
    wz[z, x] = wt[x]

    def blank(z1):
        rk[x, z1] = jnp.zeros(rk.shape[2:], BF)
        rv[x, z1] = jnp.zeros(rv.shape[2:], BF)

    loop(z, NZ, blank)

    for h in range(heads):
        cols = slice(h * HD, (h + 1) * HD)
        s = lax.dot_general(q[:, cols], kn[:, cols], NT, preferred_element_type=F32)
        top = jnp.max(s, 1, keepdims=True)
        p = jnp.exp2((s - top) * c2)
        mx[h] = jnp.broadcast_to(top, (256, HD))
        tot[h] = jnp.broadcast_to(jnp.sum(p, 1, keepdims=True), (256, HD))
        acc[:, cols] = jnp.dot(p.astype(BF), vn[:, cols], preferred_element_type=F32)

    def chunk(x1):
        ok = seen[x1][0:1, :] > 0.5
        for h in range(heads):
            cols = slice(h * HD, (h + 1) * HD)
            keys = rk[x1, :, :, cols].reshape(256, HD)
            vals = rv[x1, :, :, cols].reshape(256, HD)
            s = lax.dot_general(q[:, cols], keys, NT, preferred_element_type=F32)
            s = jnp.where(ok, s, NEG)
            old = mx[h][:, :1]
            top = jnp.maximum(old, jnp.max(s, 1, keepdims=True))
            fade = jnp.exp2((old - top) * c2)
            p = jnp.exp2((s - top) * c2)
            mx[h] = jnp.broadcast_to(top, (256, HD))
            tot[h] = tot[h] * fade + jnp.sum(p, 1, keepdims=True)
            acc[:, cols] = acc[:, cols] * fade + jnp.dot(p.astype(BF), vals, preferred_element_type=F32)

    def w_pass(zs, sem):
        @pl.when(zs // 4 != core)
        def _():
            put(wz.at[zs], ws.at[zs % 4], wcs.at[zs % 4], wcr.at[zs % 4], tp=sib)

    def ring_step(k):
        zp, zm = (z + 1) % NZ, (z + NZ - 1) % NZ
        up, dn = (z + NZ - k + 1) % NZ, (z + k - 1) % NZ
        if k > 1:
            take(wz.at[up], wpr.at[k - 2])
            take(wz.at[dn], wmr.at[k - 2])
        if k < 4:
            put(wz.at[up], wz.at[up], wps.at[k - 1], wpr.at[k - 1], slot=at(x, zp))
            put(wz.at[dn], wz.at[dn], wms.at[k - 1], wmr.at[k - 1], slot=at(x, zm))
        else:
            put(wz.at[up, pl.ds(0, 2)], wz.at[up, pl.ds(0, 2)], wps.at[3], wpr.at[3], slot=at(x, zp))
            put(wz.at[dn, pl.ds(2, 2)], wz.at[dn, pl.ds(2, 2)], wms.at[3], wmr.at[3], slot=at(x, zm))
        w_pass(up, 0)
        if k > 1:
            w_pass(dn, 0)

    for d in (1, 3, 2):
        x1 = (x + d) % NX
        take(wz.at[z, x1], w1r.at[x1])
    def fwd_k(i):
        x1 = x - 1 - i
        for d in RING:
            z2 = (z + d) % NZ
            take(kb.at[x1, z2], k1r.at[x1, z2])
            put(kb.at[x1, z2], rk.at[x1, z], k2s.at[x1, z2], k2r.at[x1, z], slot=at(x, z2))

    loop(0, x, fwd_k)
    ring_step(1)

    def own_row(z1):
        take(rk.at[x, z1], orr.at[0, z1])
        take(rv.at[x, z1], orr.at[1, z1])

    loop(0, z, own_row)
    chunk(x)

    for i, d in enumerate(RING):
        z2 = (z + d) % NZ

        def fwd_v(x2):
            take(vb.at[x2, z2], v1r.at[x2, z2])
            put(vb.at[x2, z2], rv.at[x, z2], v2s.at[x2, z2], v2r.at[x, z2], slot=at(x2, z))

        loop(x + 1, NX, fwd_v)
    ring_step(2)

    def earlier(i):
        x1 = x - 1 - i
        for z1 in range(NZ):
            take(rk.at[x1, z1], k2r.at[x1, z1])
            take(rv.at[x1, z1], v2r.at[x1, z1])
        chunk(x1)

    loop(0, x, earlier)
    for h in range(heads):
        cols = slice(h * HD, (h + 1) * HD)
        a[core, x, :, cols] = (acc[:, cols] / tot[h]).astype(BF)

    def to_sib(g):
        return remote(a.at[core, g], a.at[core, g], cs.at[g], cr.at[g], tp=sib)

    to_sib(x).start()
    put(a.at[core, x], a.at[core, x], a1s.at[0], a1r.at[0], slot=at(right, z))
    put(a.at[core, x], a.at[core, x], a1s.at[1], a1r.at[1], slot=at(left, z))

    def tile(g, zl):
        zs = core * 4 + zl
        o = lax.dot_general(wz[zs].reshape(192, 768), a[core, g], NT, preferred_element_type=F32)
        o += lax.dot_general(ws[zl].reshape(192, 768), a[1 - core, g], NT, preferred_element_type=F32)
        for p in range(NY):
            part[g, p, zl] = o[p * 48 : (p + 1) * 48].astype(BF)
        for d in (1, 3, 2):
            p = (y + d) % NY
            put(part.at[g, p, zl], got.at[g, y, zl], ys.at[g, zl, d - 1], yr.at[g, zl, d - 1], tp=p * 2 + core)

    def tiles(j0, j1, k0, k1):
        def one(j):
            g = (x + (j % 2) * 3 + (j // 2) * (1 - 2 * (j % 2)) + NX) % NX

            def two(k):
                d = (k % 2) * ((k + 1) // 2) + (1 - k % 2) * ((NZ - k // 2) % NZ)
                zs = (z + d) % NZ

                @pl.when(zs // 4 == core)
                def _():
                    if j0 == 0:
                        take(ws.at[zs % 4], wcr.at[zs % 4])
                    tile(g, zs % 4)

            loop(k0, k1, two)

        loop(j0, j1, one)

    take(a.at[1 - core, x], cr.at[x])
    tiles(0, 1, 0, 3)
    ring_step(3)
    tiles(0, 1, 3, 5)
    take(a.at[core, left], a1r.at[0])
    put(a.at[core, left, pl.ds(0, 128)], a.at[core, left, pl.ds(0, 128)], a2s.at[0], a2r.at[0], slot=at(right, z))
    to_sib(left).start()
    take(a.at[core, right], a1r.at[1])
    put(a.at[core, right, pl.ds(128, 128)], a.at[core, right, pl.ds(128, 128)], a2s.at[1], a2r.at[1], slot=at(left, z))
    to_sib(right).start()
    take(a.at[1 - core, left], cr.at[left])
    take(a.at[1 - core, right], cr.at[right])
    tiles(1, 3, 0, 5)
    ring_step(4)
    tiles(0, 1, 5, 7)
    tiles(1, 3, 5, 7)
    take(a.at[core, across, pl.ds(0, 128)], a2r.at[0])
    take(a.at[core, across, pl.ds(128, 128)], a2r.at[1])
    to_sib(across).start()
    take(a.at[1 - core, across], cr.at[across])
    tiles(3, 4, 0, 7)
    far = (z + 4) % NZ
    take(wz.at[far, pl.ds(0, 2)], wpr.at[3])
    take(wz.at[far, pl.ds(2, 2)], wmr.at[3])
    w_pass(far, 0)
    tiles(0, 1, 7, 8)
    tiles(1, 4, 7, 8)

    def reduce(g):
        s = part[g, y].astype(F32)
        for d in (1, 3, 2):
            src = (y + NY - d) % NY
            for zl in range(4):
                take(got.at[g, src, zl], yr.at[g, zl, d - 1])
            s += got[g, src].astype(F32)
        return s.astype(BF)

    for d in (3, 1, 2):
        g = (x + d) % NX
        red[g] = reduce(g)
        put(red.at[g], fin.at[x], hs.at[d - 1], hr.at[d - 1], slot=at(g, z))
    fin[x] = reduce(x)
    for d in (3, 1, 2):
        take(fin.at[(x + NX - d) % NX], hr.at[d - 1])
    for src in range(NX):
        for zs in range(4):
            flat[zs * 192 + src * 48 : zs * 192 + (src + 1) * 48, :] = fin[src, zs]
    rows = lax.broadcasted_iota(jnp.int32, (256, 256), 0)
    cols = lax.broadcasted_iota(jnp.int32, (256, 256), 1)
    eye = jnp.where(rows == cols, 1.0, 0.0).astype(BF)
    summed = lax.dot_general(eye, flat[...], NT, preferred_element_type=F32)
    out[...] = (resid[...].astype(F32) + summed).astype(BF)

    for d in (1, 3, 2):
        x2 = (x + d) % NX
        sent(wt.at[x2], w1s.at[x2])
        sent(red.at[x2], hs.at[d - 1])
    for k in range(3):
        sent(wz.at[z], wps.at[k])
        sent(wz.at[z], wms.at[k])
    sent(wz.at[z, pl.ds(0, 2)], wps.at[3])
    sent(wz.at[z, pl.ds(2, 2)], wms.at[3])
    for zl in range(4):
        sent(wz.at[z], wcs.at[zl])
    for g in range(NX):
        sent(a.at[core, g], cs.at[g])
    for i in range(2):
        sent(a.at[core, x], a1s.at[i])
        sent(a.at[core, x, pl.ds(0, 128)], a2s.at[i])

    def tile_sent(g):
        for zl in range(4):
            for d in range(3):
                sent(part.at[g, 0, zl], ys.at[g, zl, d])

    loop(0, NX, tile_sent)
    for d in RING:
        z2 = (z + d) % NZ

        @pl.when(z2 > z)
        def _():
            sent(sk.at[x, z2], os.at[0, z2])
            sent(sv.at[x, z2], os.at[1, z2])

        def given(x2):
            sent(sk.at[x2, z2], k1s.at[x2, z2])
            sent(sv.at[x2, z2], v1s.at[x2, z2])
            sent(vb.at[x2, z2], v2s.at[x2, z2])

        def passed(x1):
            sent(kb.at[x1, z2], k2s.at[x1, z2])

        loop(x + 1, NX, given)
        loop(0, x, passed)

    def straight(x2):
        sent(sk.at[x2, z], k2s.at[x2, z])
        sent(sv.at[x2, z], v2s.at[x2, z])

    loop(x + 1, NX, straight)


def per_device(queries, k_new, v_new, k_clean, v_clean, lists, counts, resid, w_out):
    width = queries.shape[1]
    wt = w_out.T.reshape(NX, 48, width)
    blocks = (-1, BLK, width)
    vm = pl.BlockSpec(memory_space=VM)
    heads = width // HD
    return pl.pallas_call(
        layer_kernel,
        out_shape=jax.ShapeDtypeStruct((256, width), BF),
        in_specs=[vm] * 9,
        out_specs=vm,
        scratch_shapes=[
            VM((NX, NZ, 32, width), BF), VM((NX, NZ, 32, width), BF),
            VM((NX, NZ, 32, width), BF), VM((NX, NZ, 32, width), BF),
            VM((NX, NZ, 32, width), BF), VM((NX, NZ, 32, width), BF),
            VM((NZ, NX, 48, width), BF), VM((4, NX, 48, width), BF), VM((NX, 8, 256), F32),
            VM((heads, 256, HD), F32), VM((heads, 256, HD), F32), VM((256, width), F32),
            VM((8, 128), jnp.int32), pltpu.SMEM((8, 128), jnp.int32),
            VM((2, NX, 256, width), BF), VM((NX, NY, 4, 48, 256), BF), VM((NX, NY, 4, 48, 256), BF),
            VM((NX, 4, 48, 256), BF), VM((NX, 4, 48, 256), BF), VM((width, 256), BF),
            DMA, DMA((NX, NZ)), DMA((NX, NZ)), DMA((NX, NZ)), DMA((NX, NZ)),
            DMA((NX, NZ)), DMA((NX, NZ)), DMA((NX, NZ)), DMA((NX, NZ)),
            DMA((2, NZ)), DMA((2, NZ)), DMA((NX,)), DMA((NX,)),
            DMA((4,)), DMA((4,)), DMA((4,)), DMA((4,)), DMA((4,)), DMA((4,)),
            DMA((NX,)), DMA((NX,)), DMA((2,)), DMA((2,)), DMA((2,)), DMA((2,)),
            DMA((NX, 4, 3)), DMA((NX, 4, 3)), DMA((3,)), DMA((3,)),
        ],
        compiler_params=pltpu.CompilerParams(
            collective_id=0, has_side_effects=True, vmem_limit_bytes=56 << 20
        ),
        name="layer",
    )(
        queries, k_new, v_new, k_clean.reshape(blocks), v_clean.reshape(blocks), wt,
        lists, counts.reshape(1, -1), resid,
    )


def solution(mesh):
    in_specs = (
        P("slot", "tp"),
        P("slot", "tp"),
        P("slot", "tp"),
        P("slot", "tp"),
        P("slot", "tp"),
        P(),
        P(),
        P("slot", "tp"),
        P("tp", "slot"),
    )
    out_specs = P("slot", "tp")
    return jax.shard_map(
        per_device, mesh=mesh, in_specs=in_specs, out_specs=out_specs, check_vma=False
    )
```

time: 418 us -> 120 us (0.29)
  waiting for transfers between devices: 295 us -> 0 us
  Pallas kernels: 0 us -> 119 us
  matrix products: 59.9 us -> 0 us
  other arithmetic: 25.1 us -> 0 us
  local copies, waits for them, and re-layouts: 22.5 us -> 1.77 us
  between operations: 13.2 us -> 0.01 us
    all_gather x3 -> x0, waiting for transfers between devices: 260 us -> none  [the longest x1 122 us: per_device(): k_piece = lax.all_gather(k_clean, 'slot', axis=0, tiled=True)]
    pallas_call x0 -> x1, Pallas kernels: none -> 119 us  [per_device(): pl.pallas_call(layer_kernel, out_shape=jax.ShapeDtypeStruct((256, width),...]
    dot_general x5 -> x0, matrix products: 59.9 us -> none  [the longest x2 24.5 us: weigh(): jnp.einsum('hqk,khd->hqd', ex.astype(jnp.bfloat16), v_three, preferred_el...]
    reduce_scatter x1 -> x0, waiting for transfers between devices: 33.2 us -> none  [per_device(): lax.psum_scatter(terms.astype(jnp.bfloat16), 'tp', scatter_dimension=1, t...]
    reduce_sum x2 -> x0, other arithmetic: 22.3 us -> none  [the longest x1 22.1 us: per_device(): jnp.sum(ex, -1)]
    all_gather x1 -> x0, local copies, waits for them, and re-layouts: 15.8 us -> none  [per_device(): v_piece = lax.all_gather(v_clean, 'slot', axis=0, tiled=True)]
  transfers between devices with their start and end apart: 4 -> 0, of which waited for: 4 -> 0; matrix products, arithmetic and copies ran while one was open for 22% -> 0% of each run, Pallas kernels for 0% -> 0%
where the time goes in v2:
time: 120 us
  Pallas kernels  119 us (99%)
  local copies, waits for them, and re-layouts  1.77 us (1%)
    pallas_call x1, Pallas kernels, per_device(): pl.pallas_call(layer_kernel, out_shape=jax.ShapeDtypeStruct((256, width),...  119 us

profile of v2, /device:TPU:1, one launch (start us, length us, event | category | flops | bytes accessed | tf_op | source)
XLA Modules:
  0.0 120.3 jit_solution(12043256316179158571)
XLA Ops:
  0.0 118.6 %layer.1 = bf16[256,768]{1,0:T(8,128)(2,1)} custom-call(bf16[256,768]{1,0:T(8,128)(2,1)} %q.1, bf16[256,768]{1,0:T(8,128)(2,1)} %kn.1, bf16[256,768]{1,0:T(8,128)(2,1)} %vn.1, bf16[16,16,768]{2,1,0:T(8,128)(2,1)} %bitcast.6, bf16[16,16,768]{2,1,0:T(8,128)(2,1)} %bitcast.7, bf16[4,48,768]{2,1,0:T(8,128)(2,1)} %bitcast.8, s32[32,62]{1,0:T(8,128)} %lists.1, ...), custom_call_target="tpu_custom_call" | custom-call | tf_op jit(solution)/shard_map/layer/pallas_call | solution.py:374
  118.6 1.8 %copy.11 = bf16[256,768]{1,0:T(8,128)(2,1)} copy(bf16[256,768]{1,0:T(8,128)(2,1)} %layer.1) | data formatting | bytes 786432

commit v3 on v2

v3 whole, which is shorter than its diff:
```python
import math

import jax
import jax.numpy as jnp
from jax import lax
from jax.experimental import pallas as pl
from jax.experimental.pallas import tpu as pltpu
from jax.sharding import PartitionSpec as P

HD = 128
BLK = 16
NX, NZ, NY = 4, 8, 4
RING = (4, 3, 5, 2, 6, 1, 7)
MESH = pl.DeviceIdType.MESH
BF = jnp.bfloat16
F32 = jnp.float32
NEG = -1e30
NT = (((1,), (1,)), ((), ()))
VM = pltpu.VMEM
DMA = pltpu.SemaphoreType.DMA


def remote(src, dst, ssem, rsem, **where):
    return pltpu.make_async_remote_copy(
        src_ref=src, dst_ref=dst, send_sem=ssem, recv_sem=rsem, device_id=where, device_id_type=MESH
    )


def loop(lo, hi, body):
    def step(i, c):
        body(i)
        return c

    lax.fori_loop(lo, hi, step, 0)


def layer_kernel(
    q_in, kn_in, vn_in, kc, vc, wt, lists, counts, res_in,
    out,
    q, kn, vn, resid, ins,
    sk, sv, kb, vb, rk, rv, wz, ws, seen, mx, tot, acc, tab, tabs,
    a, part, got, red, fin, flat,
    ts, k1s, k1r, k2s, k2r, v1s, v1r, v2s, v2r, os, orr, w1s, w1r, wps, wpr, wms, wmr, wcs, wcr,
    cs, cr, a1s, a1r, a2s, a2r, ys, yr, hs, hr,
):
    me = lax.axis_index("slot")
    tp = lax.axis_index("tp")
    x, z, y, core = me // NZ, me % NZ, tp // 2, tp % 2
    sib = tp + 1 - 2 * core
    left, right, across = (x + 3) % NX, (x + 1) % NX, (x + 2) % NX
    heads = q.shape[1] // HD
    c2 = math.log2(math.e) / math.sqrt(HD)

    def at(ax, az):
        return ax * NZ + az

    def put(src, dst, ssem, rsem, **where):
        remote(src, dst, ssem, rsem, **where).start()

    def take(dst, rsem):
        remote(dst, dst, rsem, rsem, slot=me).wait_recv()

    def sent(src, ssem):
        remote(src, src, ssem, ssem, slot=me).wait_send()

    barrier = pltpu.get_barrier_semaphore()
    for d in range(1, NX):
        pl.semaphore_signal(barrier, inc=1, device_id={"slot": at((x + d) % NX, z)}, device_id_type=MESH)
    for d in range(1, NZ):
        pl.semaphore_signal(barrier, inc=1, device_id={"slot": at(x, (z + d) % NZ)}, device_id_type=MESH)
    for d in range(1, NY):
        pl.semaphore_signal(barrier, inc=1, device_id={"tp": ((y + d) % NY) * 2 + core}, device_id_type=MESH)
    pl.semaphore_signal(barrier, inc=1, device_id={"tp": sib}, device_id_type=MESH)

    fetch = [
        pltpu.make_async_copy(src, dst, ins.at[i])
        for i, (src, dst) in enumerate(((q_in, q), (kn_in, kn), (vn_in, vn), (res_in, resid)))
    ]
    for copy in fetch:
        copy.start()

    lst = lists[...]
    readers = lst.shape[0]
    sub = lax.broadcasted_iota(jnp.int32, (readers, 128), 0)
    lane = lax.broadcasted_iota(jnp.int32, (readers, 128), 1)
    live_n = jnp.sum(jnp.where(sub[:, :readers] == lane[:, :readers], counts[...], 0), 1, keepdims=True)
    live = lax.broadcasted_iota(jnp.int32, lst.shape, 1) < live_n
    mine = live & (lst // BLK == me)
    within = lst % BLK
    lo = jnp.min(jnp.where(mine, within, BLK), 1, keepdims=True)
    hi = jnp.max(jnp.where(mine, within, 0), 1, keepdims=True)
    lo = jnp.where(lo < BLK, lo, 0)
    tab[0:1, :] = jnp.sum(jnp.where(sub == lane, lo, 0), 0, keepdims=True)
    tab[1:2, :] = jnp.sum(jnp.where(sub == lane, hi, 0), 0, keepdims=True)
    to_scalar = pltpu.make_async_copy(tab, tabs, ts)
    to_scalar.start()

    row = lists[pl.ds(me, 1), :]
    n_live = jnp.sum(jnp.where(lax.broadcasted_iota(jnp.int32, counts.shape, 1) == me, counts[...], 0), 1, keepdims=True)
    row_live = lax.broadcasted_iota(jnp.int32, row.shape, 1) < n_live
    owner = lax.broadcasted_iota(jnp.int32, lst.shape, 0)
    n_of = jnp.sum(jnp.where((row // BLK == owner) & row_live, 1, 0), 1, keepdims=True)
    for x1 in range(NX):
        key = lax.broadcasted_iota(jnp.int32, (readers, 256), 1)
        own_of = lax.broadcasted_iota(jnp.int32, (readers, 256), 0)
        cnt = jnp.sum(jnp.where(own_of == x1 * NZ + key // 32, n_of, 0), 0, keepdims=True)
        odd = (lax.broadcasted_iota(jnp.int32, (1, 256), 1) // BLK) % 2
        seen[x1] = jnp.broadcast_to(jnp.where(cnt > odd, 1.0, 0.0), (8, 256))
    to_scalar.wait()

    def pack(x2):
        for z2 in range(NZ):
            r = at(x2, z2)
            for half in range(2):
                blk = tabs[half, r]
                sk[x2, z2, half * BLK : (half + 1) * BLK, :] = kc[blk]
                sv[x2, z2, half * BLK : (half + 1) * BLK, :] = vc[blk]

    pack(x)
    pl.semaphore_wait(barrier, NX - 1 + NZ - 1 + NY - 1 + 1)

    for d in RING:
        z2 = (z + d) % NZ

        @pl.when(z2 > z)
        def _():
            put(sk.at[x, z2], rk.at[x, z], os.at[z2], orr.at[z], slot=at(x, z2))
            put(sv.at[x, z2], rv.at[x, z], os.at[z2], orr.at[z], slot=at(x, z2))

    def give(x2):
        pack(x2)
        for d in RING:
            z2 = (z + d) % NZ
            put(sv.at[x2, z2], vb.at[x2, z], v1s.at[x2], v1r.at[x2, z], slot=at(x, z2))
            put(sk.at[x2, z2], kb.at[x, z2], k1s.at[x2], k1r.at[x, z2], slot=at(x2, z))
        put(sk.at[x2, z], rk.at[x, z], k1s.at[x2], k2r.at[x], slot=at(x2, z))
        put(sv.at[x2, z], rv.at[x, z], v1s.at[x2], v2r.at[x], slot=at(x2, z))

    loop(x + 1, NX, give)
    for d in (1, 3, 2):
        x2 = (x + d) % NX
        put(wt.at[x2], wz.at[z, x], w1s.at[x2], w1r.at[x], slot=at(x2, z))
    mine_w = pltpu.make_async_copy(wt.at[x], wz.at[z, x], ins.at[4])
    mine_w.start()

    def blank(z1):
        rk[x, z1] = jnp.zeros(rk.shape[2:], BF)
        rv[x, z1] = jnp.zeros(rv.shape[2:], BF)

    loop(z, NZ, blank)

    for copy in fetch:
        copy.wait()
    mine_w.wait()
    for h in range(heads):
        cols = slice(h * HD, (h + 1) * HD)
        s = lax.dot_general(q[:, cols], kn[:, cols], NT, preferred_element_type=F32)
        top = jnp.broadcast_to(jnp.max(s, 1, keepdims=True), (256, HD))
        p = jnp.exp2((s - jnp.concatenate([top, top], 1)) * c2)
        mx[h] = top
        tot[h] = jnp.broadcast_to(jnp.sum(p, 1, keepdims=True), (256, HD))
        acc[:, cols] = jnp.dot(p.astype(BF), vn[:, cols], preferred_element_type=F32)

    def chunk(x1):
        ok = seen[x1][0:1, :] > 0.5
        for h in range(heads):
            cols = slice(h * HD, (h + 1) * HD)
            keys = rk[x1, :, :, cols].reshape(256, HD)
            vals = rv[x1, :, :, cols].reshape(256, HD)
            s = lax.dot_general(q[:, cols], keys, NT, preferred_element_type=F32)
            s = jnp.where(ok, s, NEG)
            old = mx[h]
            top = jnp.maximum(old, jnp.max(s, 1, keepdims=True))
            fade = jnp.exp2((old - top) * c2)
            p = jnp.exp2((s - jnp.concatenate([top, top], 1)) * c2)
            mx[h] = top
            tot[h] = tot[h] * fade + jnp.sum(p, 1, keepdims=True)
            acc[:, cols] = acc[:, cols] * fade + jnp.dot(p.astype(BF), vals, preferred_element_type=F32)

    def w_pass(zs, sem):
        @pl.when(zs // 4 != core)
        def _():
            put(wz.at[zs], ws.at[zs % 4], wcs.at[zs % 4], wcr.at[zs % 4], tp=sib)

    def ring_step(k):
        zp, zm = (z + 1) % NZ, (z + NZ - 1) % NZ
        up, dn = (z + NZ - k + 1) % NZ, (z + k - 1) % NZ
        if k == 1:
            for d in (1, 3, 2):
                x1 = (x + d) % NX
                take(wz.at[z, x1], w1r.at[x1])
        if k > 1:
            take(wz.at[up], wpr.at[k - 2])
            take(wz.at[dn], wmr.at[k - 2])
        if k < 4:
            put(wz.at[up], wz.at[up], wps.at[k - 1], wpr.at[k - 1], slot=at(x, zp))
            put(wz.at[dn], wz.at[dn], wms.at[k - 1], wmr.at[k - 1], slot=at(x, zm))
        else:
            put(wz.at[up, pl.ds(0, 2)], wz.at[up, pl.ds(0, 2)], wps.at[3], wpr.at[3], slot=at(x, zp))
            put(wz.at[dn, pl.ds(2, 2)], wz.at[dn, pl.ds(2, 2)], wms.at[3], wmr.at[3], slot=at(x, zm))
        w_pass(up, 0)
        if k > 1:
            w_pass(dn, 0)

    def fwd_k(i):
        x1 = x - 1 - i
        for d in RING:
            z2 = (z + d) % NZ
            take(kb.at[x1, z2], k1r.at[x1, z2])
            put(kb.at[x1, z2], rk.at[x1, z], k2s.at[x1], k2r.at[x1], slot=at(x, z2))

    loop(0, x, fwd_k)

    def own_row(z1):
        take(vb.at[0, pl.ds(0, 2)], orr.at[z1])

    loop(0, z, own_row)
    chunk(x)

    for i, d in enumerate(RING):
        z2 = (z + d) % NZ

        def fwd_v(x2):
            take(vb.at[x2, z2], v1r.at[x2, z2])
            put(vb.at[x2, z2], rv.at[x, z2], v2s.at[x2], v2r.at[x], slot=at(x2, z))

        loop(x + 1, NX, fwd_v)
        if i == 3:
            ring_step(1)
    ring_step(2)

    def earlier(i):
        x1 = x - 1 - i
        take(rk.at[x1], k2r.at[x1])
        take(rv.at[x1], v2r.at[x1])
        chunk(x1)

    loop(0, x, earlier)
    for h in range(heads):
        cols = slice(h * HD, (h + 1) * HD)
        a[core, x, :, cols] = (acc[:, cols] / tot[h]).astype(BF)

    def rows(c, g, r):
        return a.at[c, g, pl.ds(r * 128, 128)]

    def to_sib(g, r):
        put(rows(core, g, r), rows(core, g, r), cs.at[g, r], cr.at[g, r], tp=sib)

    def from_sib(g, r):
        take(rows(1 - core, g, r), cr.at[g, r])

    for r in range(2):
        put(rows(core, x, r), rows(core, x, r), a1s.at[0, r], a1r.at[0, r], slot=at(right, z))
        put(rows(core, x, 1 - r), rows(core, x, 1 - r), a1s.at[1, 1 - r], a1r.at[1, 1 - r], slot=at(left, z))
    to_sib(x, 0)
    to_sib(x, 1)

    def tile(g, zl, r, n):
        zs = core * 4 + zl
        o = lax.dot_general(wz[zs].reshape(192, 768), a[core, g, pl.ds(r * 128, n * 128)], NT, preferred_element_type=F32)
        o += lax.dot_general(ws[zl].reshape(192, 768), a[1 - core, g, pl.ds(r * 128, n * 128)], NT, preferred_element_type=F32)
        for i in range(n):
            for p in range(NY):
                part[g, r + i, p, zl] = o[p * 48 : (p + 1) * 48, i * 128 : (i + 1) * 128].astype(BF)
            for d in (1, 3, 2):
                p = (y + d) % NY
                put(
                    part.at[g, r + i, p, zl], got.at[g, r + i, y, zl],
                    ys.at[g], yr.at[g, r + i], tp=p * 2 + core,
                )

    def tiles(g, r, n, k0, k1):
        def one(k):
            d = (k % 2) * ((k + 1) // 2) + (1 - k % 2) * ((NZ - k // 2) % NZ)
            zs = (z + d) % NZ

            @pl.when(zs // 4 == core)
            def _():
                tile(g, zs % 4, r, n)

        loop(k0, k1, one)

    def w_here(k0, k1):
        def one(k):
            d = (k % 2) * ((k + 1) // 2) + (1 - k % 2) * ((NZ - k // 2) % NZ)
            zs = (z + d) % NZ

            @pl.when(zs // 4 == core)
            def _():
                take(ws.at[zs % 4], wcr.at[zs % 4])

        loop(k0, k1, one)

    def half_in(i):
        if i == 0:
            take(rows(core, left, 0), a1r.at[0, 0])
            put(rows(core, left, 0), rows(core, left, 0), a2s.at[0], a2r.at[0], slot=at(right, z))
            to_sib(left, 0)
            take(rows(core, right, 1), a1r.at[1, 1])
            put(rows(core, right, 1), rows(core, right, 1), a2s.at[1], a2r.at[1], slot=at(left, z))
            to_sib(right, 1)
        else:
            take(rows(core, left, 1), a1r.at[0, 1])
            to_sib(left, 1)
            take(rows(core, right, 0), a1r.at[1, 0])
            to_sib(right, 0)

    for r in range(2):
        from_sib(x, r)
    w_here(0, 3)
    tiles(x, 0, 2, 0, 3)
    half_in(0)
    ring_step(3)
    w_here(3, 5)
    tiles(x, 0, 2, 3, 5)
    from_sib(left, 0)
    tiles(left, 0, 1, 0, 5)
    from_sib(right, 1)
    tiles(right, 1, 1, 0, 5)
    half_in(1)
    from_sib(left, 1)
    tiles(left, 1, 1, 0, 5)
    from_sib(right, 0)
    tiles(right, 0, 1, 0, 5)
    ring_step(4)
    w_here(5, 7)
    tiles(x, 0, 2, 5, 7)
    tiles(left, 0, 2, 5, 7)
    tiles(right, 0, 2, 5, 7)
    take(rows(core, across, 0), a2r.at[0])
    to_sib(across, 0)
    take(rows(core, across, 1), a2r.at[1])
    to_sib(across, 1)
    for r in range(2):
        from_sib(across, r)
    tiles(across, 0, 2, 0, 7)
    far = (z + 4) % NZ
    take(wz.at[far, pl.ds(0, 2)], wpr.at[3])
    take(wz.at[far, pl.ds(2, 2)], wmr.at[3])
    w_pass(far, 0)
    w_here(7, 8)
    for g in (across, left, right, x):
        tiles(g, 0, 2, 7, 8)

    def reduce(g, r):
        take(got.at[g, r, pl.ds(0, 3)], yr.at[g, r])
        s = part[g, r, y].astype(F32)
        for d in (1, 3, 2):
            src = (y + NY - d) % NY
            s += got[g, r, src].astype(F32)
        return s.astype(BF)

    for d in (3, 1, 2):
        g = (x + d) % NX
        for r in range(2):
            red[g, r] = reduce(g, r)
        put(red.at[g], fin.at[x], hs.at[d - 1], hr.at[d - 1], slot=at(g, z))
    for r in range(2):
        fin[x, r] = reduce(x, r)
    for d in (3, 1, 2):
        take(fin.at[(x + NX - d) % NX], hr.at[d - 1])
    for src in range(NX):
        for zs in range(4):
            for r in range(2):
                flat[zs * 192 + src * 48 : zs * 192 + (src + 1) * 48, r * 128 : (r + 1) * 128] = fin[src, r, zs]
    sub = lax.broadcasted_iota(jnp.int32, (256, 256), 0)
    lane = lax.broadcasted_iota(jnp.int32, (256, 256), 1)
    eye = jnp.where(sub == lane, 1.0, 0.0).astype(BF)
    summed = lax.dot_general(eye, flat[...], NT, preferred_element_type=F32)
    out[...] = (resid[...].astype(F32) + summed).astype(BF)

    for d in (1, 3, 2):
        x2 = (x + d) % NX
        sent(wt.at[x2], w1s.at[x2])
        sent(red.at[x2], hs.at[d - 1])
    for k in range(3):
        sent(wz.at[z], wps.at[k])
        sent(wz.at[z], wms.at[k])
    sent(wz.at[z, pl.ds(0, 2)], wps.at[3])
    sent(wz.at[z, pl.ds(2, 2)], wms.at[3])
    for zl in range(4):
        sent(wz.at[z], wcs.at[zl])
    for r in range(2):
        for g in range(NX):
            sent(rows(core, x, r), cs.at[g, r])
        for i in range(2):
            sent(rows(core, x, r), a1s.at[i, r])
        sent(rows(core, x, r), a2s.at[r])

    for g in range(NX):
        sent(part.at[g, pl.ds(0, 2), pl.ds(0, 3)], ys.at[g])

    def row_sent(z2):
        sent(sk.at[x, pl.ds(0, 2)], os.at[z2])

    def given(x2):
        sent(sk.at[x2], k1s.at[x2])
        sent(sv.at[x2], v1s.at[x2])
        sent(vb.at[x2, pl.ds(0, NZ - 1)], v2s.at[x2])

    def passed(x1):
        sent(kb.at[x1, pl.ds(0, NZ - 1)], k2s.at[x1])

    loop(z + 1, NZ, row_sent)
    loop(x + 1, NX, given)
    loop(0, x, passed)


def per_device(queries, k_new, v_new, k_clean, v_clean, lists, counts, resid, w_out):
    width = queries.shape[1]
    wt = w_out.T.reshape(NX, 48, width)
    blocks = (-1, BLK, width)
    vm, hbm = pl.BlockSpec(memory_space=VM), pl.BlockSpec(memory_space=pl.ANY)
    heads = width // HD
    return pl.pallas_call(
        layer_kernel,
        out_shape=jax.ShapeDtypeStruct((256, width), BF),
        in_specs=[hbm] * 3 + [vm] * 2 + [hbm] + [vm] * 2 + [hbm],
        out_specs=vm,
        scratch_shapes=[
            VM((256, width), BF), VM((256, width), BF), VM((256, width), BF), VM((256, width), BF), DMA((5,)),
            VM((NX, NZ, 32, width), BF), VM((NX, NZ, 32, width), BF),
            VM((NX, NZ, 32, width), BF), VM((NX, NZ, 32, width), BF),
            VM((NX, NZ, 32, width), BF), VM((NX, NZ, 32, width), BF),
            VM((NZ, NX, 48, width), BF), VM((4, NX, 48, width), BF), VM((NX, 8, 256), F32),
            VM((heads, 256, HD), F32), VM((heads, 256, HD), F32), VM((256, width), F32),
            VM((8, 128), jnp.int32), pltpu.SMEM((8, 128), jnp.int32),
            VM((2, NX, 256, width), BF), VM((NX, 2, NY, 4, 48, 128), BF), VM((NX, 2, NY, 4, 48, 128), BF),
            VM((NX, 2, 4, 48, 128), BF), VM((NX, 2, 4, 48, 128), BF), VM((width, 256), BF),
            DMA, DMA((NX,)), DMA((NX, NZ)), DMA((NX,)), DMA((NX,)),
            DMA((NX,)), DMA((NX, NZ)), DMA((NX,)), DMA((NX,)),
            DMA((NZ,)), DMA((NZ,)), DMA((NX,)), DMA((NX,)),
            DMA((4,)), DMA((4,)), DMA((4,)), DMA((4,)), DMA((4,)), DMA((4,)),
            DMA((NX, 2)), DMA((NX, 2)), DMA((2, 2)), DMA((2, 2)), DMA((2,)), DMA((2,)),
            DMA((NX,)), DMA((NX, 2)), DMA((3,)), DMA((3,)),
        ],
        compiler_params=pltpu.CompilerParams(
            collective_id=0, has_side_effects=True, vmem_limit_bytes=56 << 20
        ),
        name="layer",
    )(
        queries, k_new, v_new, k_clean.reshape(blocks), v_clean.reshape(blocks), wt,
        lists, counts.reshape(1, -1), resid,
    )


def solution(mesh):
    in_specs = (
        P("slot", "tp"),
        P("slot", "tp"),
        P("slot", "tp"),
        P("slot", "tp"),
        P("slot", "tp"),
        P(),
        P(),
        P("slot", "tp"),
        P("tp", "slot"),
    )
    out_specs = P("slot", "tp")
    return jax.shard_map(
        per_device, mesh=mesh, in_specs=in_specs, out_specs=out_specs, check_vma=False
    )
```

time: 120 us -> 103 us (0.86)
  Pallas kernels: 119 us -> 101 us
    pallas_call x1, Pallas kernels: 119 us -> 101 us  [per_device(): pl.pallas_call(layer_kernel, out_shape=jax.ShapeDtypeStruct((256, width),...]
where the time goes in v3:
time: 103 us
  Pallas kernels  101 us (98%)
  local copies, waits for them, and re-layouts  1.77 us (2%)
    pallas_call x1, Pallas kernels, per_device(): pl.pallas_call(layer_kernel, out_shape=jax.ShapeDtypeStruct((256, width),...  101 us

profile of v3, /device:TPU:1, one launch (start us, length us, event | category | flops | bytes accessed | tf_op | source)
XLA Modules:
  0.0 102.7 jit_solution(13269136580164213760)
XLA Ops:
  0.0 100.9 %layer.1 = bf16[256,768]{1,0:T(8,128)(2,1)} custom-call(bf16[256,768]{1,0:T(8,128)(2,1)} %q_in.1, bf16[256,768]{1,0:T(8,128)(2,1)} %kn_in.1, bf16[256,768]{1,0:T(8,128)(2,1)} %vn_in.1, bf16[16,16,768]{2,1,0:T(8,128)(2,1)} %bitcast.6, bf16[16,16,768]{2,1,0:T(8,128)(2,1)} %bitcast.7, bf16[4,48,768]{2,1,0:T(8,128)(2,1)} %bitcast.8, s32[32,62]{1,0:T(8,128)} %lists.1, ...), custom_call_target="tpu_custom_call" | custom-call | tf_op jit(solution)/shard_map/layer/pallas_call | solution.py:415
  100.9 1.8 %copy.11 = bf16[256,768]{1,0:T(8,128)(2,1)} copy(bf16[256,768]{1,0:T(8,128)(2,1)} %layer.1) | data formatting | bytes 786432

commit v4 on v3

--- a/solution.py
+++ b/solution.py
@@ -1,3 +1,4 @@
+import functools
 import math
 
 import jax
@@ -10,7 +11,7 @@
 HD = 128
 BLK = 16
 NX, NZ, NY = 4, 8, 4
-RING = (4, 3, 5, 2, 6, 1, 7)
+FAR, NEAR = (4, 3, 5), (2, 6, 1, 7)
 MESH = pl.DeviceIdType.MESH
 BF = jnp.bfloat16
 F32 = jnp.float32
@@ -35,9 +36,9 @@
 
 
 def layer_kernel(
-    q_in, kn_in, vn_in, kc, vc, wt, lists, counts, res_in,
+    q_in, kn_in, vn_in, kc_in, vc_in, wt, lists, counts, res_in,
     out,
-    q, kn, vn, resid, ins,
+    q, kn, vn, resid, kc, vc, ins,
     sk, sv, kb, vb, rk, rv, wz, ws, seen, mx, tot, acc, tab, tabs,
     a, part, got, red, fin, flat,
     ts, k1s, k1r, k2s, k2r, v1s, v1r, v2s, v2r, os, orr, w1s, w1r, wps, wpr, wms, wmr, wcs, wcr,
@@ -72,6 +73,9 @@
         pl.semaphore_signal(barrier, inc=1, device_id={"tp": ((y + d) % NY) * 2 + core}, device_id_type=MESH)
     pl.semaphore_signal(barrier, inc=1, device_id={"tp": sib}, device_id_type=MESH)
 
+    blocks = [pltpu.make_async_copy(kc_in, kc, ins.at[5]), pltpu.make_async_copy(vc_in, vc, ins.at[6])]
+    for copy in blocks:
+        copy.start()
     fetch = [
         pltpu.make_async_copy(src, dst, ins.at[i])
         for i, (src, dst) in enumerate(((q_in, q), (kn_in, kn), (vn_in, vn), (res_in, resid)))
@@ -116,27 +120,44 @@
                 sk[x2, z2, half * BLK : (half + 1) * BLK, :] = kc[blk]
                 sv[x2, z2, half * BLK : (half + 1) * BLK, :] = vc[blk]
 
+    for copy in blocks:
+        copy.wait()
     pack(x)
     pl.semaphore_wait(barrier, NX - 1 + NZ - 1 + NY - 1 + 1)
 
-    for d in RING:
-        z2 = (z + d) % NZ
-
-        @pl.when(z2 > z)
-        def _():
-            put(sk.at[x, z2], rk.at[x, z], os.at[z2], orr.at[z], slot=at(x, z2))
-            put(sv.at[x, z2], rv.at[x, z], os.at[z2], orr.at[z], slot=at(x, z2))
+    def give_row(ds):
+        for d in ds:
+            z2 = (z + d) % NZ
+
+            @pl.when(z2 > z)
+            def _():
+                put(sk.at[x, z2], rk.at[x, z], os.at[z2], orr.at[z], slot=at(x, z2))
+                put(sv.at[x, z2], rv.at[x, z], os.at[z2], orr.at[z], slot=at(x, z2))
+
+    def give_v(ds, x2):
+        for d in ds:
+            z2 = (z + d) % NZ
+            put(sv.at[x2, z2], vb.at[x2, z], v1s.at[x2], v1r.at[x2, z], slot=at(x, z2))
 
     def give(x2):
         pack(x2)
-        for d in RING:
+        for d in FAR:
             z2 = (z + d) % NZ
             put(sv.at[x2, z2], vb.at[x2, z], v1s.at[x2], v1r.at[x2, z], slot=at(x, z2))
             put(sk.at[x2, z2], kb.at[x, z2], k1s.at[x2], k1r.at[x, z2], slot=at(x2, z))
+
+    def give_k(x2):
+        for d in NEAR:
+            z2 = (z + d) % NZ
+            put(sk.at[x2, z2], kb.at[x, z2], k1s.at[x2], k1r.at[x, z2], slot=at(x2, z))
         put(sk.at[x2, z], rk.at[x, z], k1s.at[x2], k2r.at[x], slot=at(x2, z))
+
+    def give_rest(x2):
         put(sv.at[x2, z], rv.at[x, z], v1s.at[x2], v2r.at[x], slot=at(x2, z))
 
+    give_row(FAR)
     loop(x + 1, NX, give)
+    loop(x + 1, NX, give_k)
     for d in (1, 3, 2):
         x2 = (x + d) % NX
         put(wt.at[x2], wz.at[z, x], w1s.at[x2], w1r.at[x], slot=at(x2, z))
@@ -202,14 +223,18 @@
         if k > 1:
             w_pass(dn, 0)
 
-    def fwd_k(i):
+    def fwd_k(ds, i):
         x1 = x - 1 - i
-        for d in RING:
+        for d in ds:
             z2 = (z + d) % NZ
             take(kb.at[x1, z2], k1r.at[x1, z2])
             put(kb.at[x1, z2], rk.at[x1, z], k2s.at[x1], k2r.at[x1], slot=at(x, z2))
 
-    loop(0, x, fwd_k)
+    give_row(NEAR)
+    loop(x + 1, NX, functools.partial(give_v, NEAR))
+    loop(x + 1, NX, give_rest)
+    loop(0, x, functools.partial(fwd_k, FAR))
+    loop(0, x, functools.partial(fwd_k, NEAR))
 
     def own_row(z1):
         take(vb.at[0, pl.ds(0, 2)], orr.at[z1])
@@ -217,7 +242,7 @@
     loop(0, z, own_row)
     chunk(x)
 
-    for i, d in enumerate(RING):
+    for i, d in enumerate(FAR + NEAR):
         z2 = (z + d) % NZ
 
         def fwd_v(x2):
@@ -225,7 +250,7 @@
             put(vb.at[x2, z2], rv.at[x, z2], v2s.at[x2], v2r.at[x], slot=at(x2, z))
 
         loop(x + 1, NX, fwd_v)
-        if i == 3:
+        if i == 2:
             ring_step(1)
     ring_step(2)
 
@@ -254,6 +279,7 @@
         put(rows(core, x, 1 - r), rows(core, x, 1 - r), a1s.at[1, 1 - r], a1r.at[1, 1 - r], slot=at(left, z))
     to_sib(x, 0)
     to_sib(x, 1)
+    ring_step(3)
 
     def tile(g, zl, r, n):
         zs = core * 4 + zl
@@ -310,7 +336,6 @@
     w_here(0, 3)
     tiles(x, 0, 2, 0, 3)
     half_in(0)
-    ring_step(3)
     w_here(3, 5)
     tiles(x, 0, 2, 3, 5)
     from_sib(left, 0)
@@ -415,10 +440,11 @@
     return pl.pallas_call(
         layer_kernel,
         out_shape=jax.ShapeDtypeStruct((256, width), BF),
-        in_specs=[hbm] * 3 + [vm] * 2 + [hbm] + [vm] * 2 + [hbm],
+        in_specs=[hbm] * 6 + [vm] * 2 + [hbm],
         out_specs=vm,
         scratch_shapes=[
-            VM((256, width), BF), VM((256, width), BF), VM((256, width), BF), VM((256, width), BF), DMA((5,)),
+            VM((256, width), BF), VM((256, width), BF), VM((256, width), BF), VM((256, width), BF),
+            VM((256 // BLK, BLK, width), BF), VM((256 // BLK, BLK, width), BF), DMA((7,)),
             VM((NX, NZ, 32, width), BF), VM((NX, NZ, 32, width), BF),
             VM((NX, NZ, 32, width), BF), VM((NX, NZ, 32, width), BF),
             VM((NX, NZ, 32, width), BF), VM((NX, NZ, 32, width), BF),

time: 103 us -> 101 us (0.981)
  Pallas kernels: 101 us -> 98.5 us
    pallas_call x1, Pallas kernels: 101 us -> 98.5 us  [per_device(): pl.pallas_call(layer_kernel, out_shape=jax.ShapeDtypeStruct((256, width),...]
where the time goes in v4:
time: 101 us; the launch traced here: 100 us
  Pallas kernels  98.5 us (98%)
  local copies, waits for them, and re-layouts  1.77 us (2%)
    pallas_call x1, Pallas kernels, per_device(): pl.pallas_call(layer_kernel, out_shape=jax.ShapeDtypeStruct((256, width),...  98.5 us

profile of v4, /device:TPU:1, one launch (start us, length us, event | category | flops | bytes accessed | tf_op | source)
XLA Modules:
  0.0 100.3 jit_solution(11897556954142900348)
XLA Ops:
  0.0 98.5 %layer.1 = bf16[256,768]{1,0:T(8,128)(2,1)} custom-call(bf16[256,768]{1,0:T(8,128)(2,1)} %q_in.1, bf16[256,768]{1,0:T(8,128)(2,1)} %kn_in.1, bf16[256,768]{1,0:T(8,128)(2,1)} %vn_in.1, bf16[16,16,768]{2,1,0:T(8,128)(2,1)} %bitcast.6, bf16[16,16,768]{2,1,0:T(8,128)(2,1)} %bitcast.7, bf16[4,48,768]{2,1,0:T(8,128)(2,1)} %bitcast.8, s32[32,62]{1,0:T(8,128)} %lists.1, ...), custom_call_target="tpu_custom_call" | custom-call | tf_op jit(solution)/shard_map/layer/pallas_call | solution.py:440
  98.5 1.8 %copy.11 = bf16[256,768]{1,0:T(8,128)(2,1)} copy(bf16[256,768]{1,0:T(8,128)(2,1)} %layer.1) | data formatting | bytes 786432

commit v5 on v4

--- a/solution.py
+++ b/solution.py
@@ -144,12 +144,12 @@
         for d in FAR:
             z2 = (z + d) % NZ
             put(sv.at[x2, z2], vb.at[x2, z], v1s.at[x2], v1r.at[x2, z], slot=at(x, z2))
-            put(sk.at[x2, z2], kb.at[x, z2], k1s.at[x2], k1r.at[x, z2], slot=at(x2, z))
+            put(sk.at[x2, z2], kb.at[x, z2], k1s.at[x2], k1r.at[x, 0], slot=at(x2, z))
 
     def give_k(x2):
         for d in NEAR:
             z2 = (z + d) % NZ
-            put(sk.at[x2, z2], kb.at[x, z2], k1s.at[x2], k1r.at[x, z2], slot=at(x2, z))
+            put(sk.at[x2, z2], kb.at[x, z2], k1s.at[x2], k1r.at[x, 1], slot=at(x2, z))
         put(sk.at[x2, z], rk.at[x, z], k1s.at[x2], k2r.at[x], slot=at(x2, z))
 
     def give_rest(x2):
@@ -160,7 +160,7 @@
     loop(x + 1, NX, give_k)
     for d in (1, 3, 2):
         x2 = (x + d) % NX
-        put(wt.at[x2], wz.at[z, x], w1s.at[x2], w1r.at[x], slot=at(x2, z))
+        put(wt.at[x2], wz.at[z, x], w1s.at[0], w1r.at[0], slot=at(x2, z))
     mine_w = pltpu.make_async_copy(wt.at[x], wz.at[z, x], ins.at[4])
     mine_w.start()
 
@@ -201,33 +201,31 @@
     def w_pass(zs, sem):
         @pl.when(zs // 4 != core)
         def _():
-            put(wz.at[zs], ws.at[zs % 4], wcs.at[zs % 4], wcr.at[zs % 4], tp=sib)
+            put(wz.at[zs], ws.at[zs % 4], wcs.at[0], wcr.at[zs % 4], tp=sib)
 
     def ring_step(k):
         zp, zm = (z + 1) % NZ, (z + NZ - 1) % NZ
         up, dn = (z + NZ - k + 1) % NZ, (z + k - 1) % NZ
         if k == 1:
-            for d in (1, 3, 2):
-                x1 = (x + d) % NX
-                take(wz.at[z, x1], w1r.at[x1])
+            take(ws.at[0, pl.ds(0, 3)], w1r.at[0])
         if k > 1:
             take(wz.at[up], wpr.at[k - 2])
             take(wz.at[dn], wmr.at[k - 2])
         if k < 4:
-            put(wz.at[up], wz.at[up], wps.at[k - 1], wpr.at[k - 1], slot=at(x, zp))
-            put(wz.at[dn], wz.at[dn], wms.at[k - 1], wmr.at[k - 1], slot=at(x, zm))
+            put(wz.at[up], wz.at[up], wps.at[0], wpr.at[k - 1], slot=at(x, zp))
+            put(wz.at[dn], wz.at[dn], wms.at[0], wmr.at[k - 1], slot=at(x, zm))
         else:
-            put(wz.at[up, pl.ds(0, 2)], wz.at[up, pl.ds(0, 2)], wps.at[3], wpr.at[3], slot=at(x, zp))
-            put(wz.at[dn, pl.ds(2, 2)], wz.at[dn, pl.ds(2, 2)], wms.at[3], wmr.at[3], slot=at(x, zm))
+            put(wz.at[up, pl.ds(0, 2)], wz.at[up, pl.ds(0, 2)], wps.at[1], wpr.at[3], slot=at(x, zp))
+            put(wz.at[dn, pl.ds(2, 2)], wz.at[dn, pl.ds(2, 2)], wms.at[1], wmr.at[3], slot=at(x, zm))
         w_pass(up, 0)
         if k > 1:
             w_pass(dn, 0)
 
     def fwd_k(ds, i):
         x1 = x - 1 - i
+        take(kb.at[x1, pl.ds(0, len(ds))], k1r.at[x1, 0 if ds is FAR else 1])
         for d in ds:
             z2 = (z + d) % NZ
-            take(kb.at[x1, z2], k1r.at[x1, z2])
             put(kb.at[x1, z2], rk.at[x1, z], k2s.at[x1], k2r.at[x1], slot=at(x, z2))
 
     give_row(NEAR)
@@ -269,14 +267,14 @@
         return a.at[c, g, pl.ds(r * 128, 128)]
 
     def to_sib(g, r):
-        put(rows(core, g, r), rows(core, g, r), cs.at[g, r], cr.at[g, r], tp=sib)
+        put(rows(core, g, r), rows(core, g, r), cs.at[0], cr.at[g, r], tp=sib)
 
     def from_sib(g, r):
         take(rows(1 - core, g, r), cr.at[g, r])
 
     for r in range(2):
-        put(rows(core, x, r), rows(core, x, r), a1s.at[0, r], a1r.at[0, r], slot=at(right, z))
-        put(rows(core, x, 1 - r), rows(core, x, 1 - r), a1s.at[1, 1 - r], a1r.at[1, 1 - r], slot=at(left, z))
+        put(rows(core, x, r), rows(core, x, r), a1s.at[0], a1r.at[0, r], slot=at(right, z))
+        put(rows(core, x, 1 - r), rows(core, x, 1 - r), a1s.at[0], a1r.at[1, 1 - r], slot=at(left, z))
     to_sib(x, 0)
     to_sib(x, 1)
     ring_step(3)
@@ -288,11 +286,11 @@
         for i in range(n):
             for p in range(NY):
                 part[g, r + i, p, zl] = o[p * 48 : (p + 1) * 48, i * 128 : (i + 1) * 128].astype(BF)
-            for d in (1, 3, 2):
+            for d in (2, 1, 3):
                 p = (y + d) % NY
                 put(
                     part.at[g, r + i, p, zl], got.at[g, r + i, y, zl],
-                    ys.at[g], yr.at[g, r + i], tp=p * 2 + core,
+                    ys.at[0], yr.at[g, r + i], tp=p * 2 + core,
                 )
 
     def tiles(g, r, n, k0, k1):
@@ -320,10 +318,10 @@
     def half_in(i):
         if i == 0:
             take(rows(core, left, 0), a1r.at[0, 0])
-            put(rows(core, left, 0), rows(core, left, 0), a2s.at[0], a2r.at[0], slot=at(right, z))
+            put(rows(core, left, 0), rows(core, left, 0), a1s.at[0], a2r.at[0], slot=at(right, z))
             to_sib(left, 0)
             take(rows(core, right, 1), a1r.at[1, 1])
-            put(rows(core, right, 1), rows(core, right, 1), a2s.at[1], a2r.at[1], slot=at(left, z))
+            put(rows(core, right, 1), rows(core, right, 1), a1s.at[0], a2r.at[1], slot=at(left, z))
             to_sib(right, 1)
         else:
             take(rows(core, left, 1), a1r.at[0, 1])
@@ -345,9 +343,9 @@
     half_in(1)
     from_sib(left, 1)
     tiles(left, 1, 1, 0, 5)
+    ring_step(4)
     from_sib(right, 0)
     tiles(right, 0, 1, 0, 5)
-    ring_step(4)
     w_here(5, 7)
     tiles(x, 0, 2, 5, 7)
     tiles(left, 0, 2, 5, 7)
@@ -379,11 +377,10 @@
         g = (x + d) % NX
         for r in range(2):
             red[g, r] = reduce(g, r)
-        put(red.at[g], fin.at[x], hs.at[d - 1], hr.at[d - 1], slot=at(g, z))
+        put(red.at[g], fin.at[x], hs.at[0], hr.at[0], slot=at(g, z))
     for r in range(2):
         fin[x, r] = reduce(x, r)
-    for d in (3, 1, 2):
-        take(fin.at[(x + NX - d) % NX], hr.at[d - 1])
+    take(red.at[pl.ds(0, 3)], hr.at[0])
     for src in range(NX):
         for zs in range(4):
             for r in range(2):
@@ -394,26 +391,16 @@
     summed = lax.dot_general(eye, flat[...], NT, preferred_element_type=F32)
     out[...] = (resid[...].astype(F32) + summed).astype(BF)
 
-    for d in (1, 3, 2):
-        x2 = (x + d) % NX
-        sent(wt.at[x2], w1s.at[x2])
-        sent(red.at[x2], hs.at[d - 1])
-    for k in range(3):
-        sent(wz.at[z], wps.at[k])
-        sent(wz.at[z], wms.at[k])
-    sent(wz.at[z, pl.ds(0, 2)], wps.at[3])
-    sent(wz.at[z, pl.ds(2, 2)], wms.at[3])
-    for zl in range(4):
-        sent(wz.at[z], wcs.at[zl])
-    for r in range(2):
-        for g in range(NX):
-            sent(rows(core, x, r), cs.at[g, r])
-        for i in range(2):
-            sent(rows(core, x, r), a1s.at[i, r])
-        sent(rows(core, x, r), a2s.at[r])
-
-    for g in range(NX):
-        sent(part.at[g, pl.ds(0, 2), pl.ds(0, 3)], ys.at[g])
+    sent(ws.at[0, pl.ds(0, 3)], w1s.at[0])
+    sent(red.at[pl.ds(0, 3)], hs.at[0])
+    sent(wz.at[pl.ds(0, 3)], wps.at[0])
+    sent(wz.at[pl.ds(0, 3)], wms.at[0])
+    sent(wz.at[z, pl.ds(0, 2)], wps.at[1])
+    sent(wz.at[z, pl.ds(2, 2)], wms.at[1])
+    sent(wz.at[pl.ds(0, 4)], wcs.at[0])
+    sent(a.at[core], cs.at[0])
+    sent(a.at[core, pl.ds(0, 3)], a1s.at[0])
+    sent(part.at[:, :, pl.ds(0, 3)], ys.at[0])
 
     def row_sent(z2):
         sent(sk.at[x, pl.ds(0, 2)], os.at[z2])
@@ -453,12 +440,12 @@
             VM((8, 128), jnp.int32), pltpu.SMEM((8, 128), jnp.int32),
             VM((2, NX, 256, width), BF), VM((NX, 2, NY, 4, 48, 128), BF), VM((NX, 2, NY, 4, 48, 128), BF),
             VM((NX, 2, 4, 48, 128), BF), VM((NX, 2, 4, 48, 128), BF), VM((width, 256), BF),
-            DMA, DMA((NX,)), DMA((NX, NZ)), DMA((NX,)), DMA((NX,)),
+            DMA, DMA((NX,)), DMA((NX, 2)), DMA((NX,)), DMA((NX,)),
             DMA((NX,)), DMA((NX, NZ)), DMA((NX,)), DMA((NX,)),
-            DMA((NZ,)), DMA((NZ,)), DMA((NX,)), DMA((NX,)),
-            DMA((4,)), DMA((4,)), DMA((4,)), DMA((4,)), DMA((4,)), DMA((4,)),
-            DMA((NX, 2)), DMA((NX, 2)), DMA((2, 2)), DMA((2, 2)), DMA((2,)), DMA((2,)),
-            DMA((NX,)), DMA((NX, 2)), DMA((3,)), DMA((3,)),
+            DMA((NZ,)), DMA((NZ,)), DMA((1,)), DMA((1,)),
+            DMA((2,)), DMA((4,)), DMA((2,)), DMA((4,)), DMA((1,)), DMA((4,)),
+            DMA((1,)), DMA((NX, 2)), DMA((1,)), DMA((2, 2)), DMA((1,)), DMA((2,)),
+            DMA((1,)), DMA((NX, 2)), DMA((1,)), DMA((1,)),
         ],
         compiler_params=pltpu.CompilerParams(
             collective_id=0, has_side_effects=True, vmem_limit_bytes=56 << 20

time: 101 us -> 99.4 us (0.984)
  Pallas kernels: 98.5 us -> 97.4 us
    pallas_call x1, Pallas kernels: 98.5 us -> 97.4 us  [per_device(): pl.pallas_call(layer_kernel, out_shape=jax.ShapeDtypeStruct((256, width),...]
where the time goes in v5:
time: 99.4 us; the launch traced here: 99.2 us
  Pallas kernels  97.4 us (98%)
  local copies, waits for them, and re-layouts  1.77 us (2%)
    pallas_call x1, Pallas kernels, per_device(): pl.pallas_call(layer_kernel, out_shape=jax.ShapeDtypeStruct((256, width),...  97.4 us

profile of v5, /device:TPU:1, one launch (start us, length us, event | category | flops | bytes accessed | tf_op | source)
XLA Modules:
  0.0 99.2 jit_solution(16466068980540550428)
XLA Ops:
  0.0 97.4 %layer.1 = bf16[256,768]{1,0:T(8,128)(2,1)} custom-call(bf16[256,768]{1,0:T(8,128)(2,1)} %q_in.1, bf16[256,768]{1,0:T(8,128)(2,1)} %kn_in.1, bf16[256,768]{1,0:T(8,128)(2,1)} %vn_in.1, bf16[16,16,768]{2,1,0:T(8,128)(2,1)} %bitcast.6, bf16[16,16,768]{2,1,0:T(8,128)(2,1)} %bitcast.7, bf16[4,48,768]{2,1,0:T(8,128)(2,1)} %bitcast.8, s32[32,62]{1,0:T(8,128)} %lists.1, ...), custom_call_target="tpu_custom_call" | custom-call | tf_op jit(solution)/shard_map/layer/pallas_call | solution.py:427
  97.4 1.8 %copy.11 = bf16[256,768]{1,0:T(8,128)(2,1)} copy(bf16[256,768]{1,0:T(8,128)(2,1)} %layer.1) | data formatting | bytes 786432

commit v6 on v5

--- a/solution.py
+++ b/solution.py
@@ -11,6 +11,7 @@
 HD = 128
 BLK = 16
 NX, NZ, NY = 4, 8, 4
+PAIR = {4: 0, 3: 1, 5: 1, 2: 2, 6: 2, 1: 3, 7: 3}
 FAR, NEAR = (4, 3, 5), (2, 6, 1, 7)
 MESH = pl.DeviceIdType.MESH
 BF = jnp.bfloat16
@@ -137,13 +138,13 @@
     def give_v(ds, x2):
         for d in ds:
             z2 = (z + d) % NZ
-            put(sv.at[x2, z2], vb.at[x2, z], v1s.at[x2], v1r.at[x2, z], slot=at(x, z2))
+            put(sv.at[x2, z2], vb.at[x2, z], v1s.at[x2], v1r.at[x2, PAIR[d]], slot=at(x, z2))
 
     def give(x2):
         pack(x2)
         for d in FAR:
             z2 = (z + d) % NZ
-            put(sv.at[x2, z2], vb.at[x2, z], v1s.at[x2], v1r.at[x2, z], slot=at(x, z2))
+            put(sv.at[x2, z2], vb.at[x2, z], v1s.at[x2], v1r.at[x2, PAIR[d]], slot=at(x, z2))
             put(sk.at[x2, z2], kb.at[x, z2], k1s.at[x2], k1r.at[x, 0], slot=at(x2, z))
 
     def give_k(x2):
@@ -244,7 +245,8 @@
         z2 = (z + d) % NZ
 
         def fwd_v(x2):
-            take(vb.at[x2, z2], v1r.at[x2, z2])
+            if d in (4, 3, 2, 1):
+                take(vb.at[x2, pl.ds(0, 1 if d == 4 else 2)], v1r.at[x2, PAIR[d]])
             put(vb.at[x2, z2], rv.at[x, z2], v2s.at[x2], v2r.at[x], slot=at(x2, z))
 
         loop(x + 1, NX, fwd_v)
@@ -441,7 +443,7 @@
             VM((2, NX, 256, width), BF), VM((NX, 2, NY, 4, 48, 128), BF), VM((NX, 2, NY, 4, 48, 128), BF),
             VM((NX, 2, 4, 48, 128), BF), VM((NX, 2, 4, 48, 128), BF), VM((width, 256), BF),
             DMA, DMA((NX,)), DMA((NX, 2)), DMA((NX,)), DMA((NX,)),
-            DMA((NX,)), DMA((NX, NZ)), DMA((NX,)), DMA((NX,)),
+            DMA((NX,)), DMA((NX, 4)), DMA((NX,)), DMA((NX,)),
             DMA((NZ,)), DMA((NZ,)), DMA((1,)), DMA((1,)),
             DMA((2,)), DMA((4,)), DMA((2,)), DMA((4,)), DMA((1,)), DMA((4,)),
             DMA((1,)), DMA((NX, 2)), DMA((1,)), DMA((2, 2)), DMA((1,)), DMA((2,)),

time: 99.4 us -> 99.3 us (level)
  no operation moved by 1% of the time
where the time goes in v6:
time: 99.3 us; the launch traced here: 99.1 us
  Pallas kernels  97.3 us (98%)
  local copies, waits for them, and re-layouts  1.77 us (2%)
    pallas_call x1, Pallas kernels, per_device(): pl.pallas_call(layer_kernel, out_shape=jax.ShapeDtypeStruct((256, width),...  97.3 us

profile of v6, /device:TPU:1, one launch (start us, length us, event | category | flops | bytes accessed | tf_op | source)
XLA Modules:
  0.0 99.1 jit_solution(286294484952150559)
XLA Ops:
  0.0 97.3 %layer.1 = bf16[256,768]{1,0:T(8,128)(2,1)} custom-call(bf16[256,768]{1,0:T(8,128)(2,1)} %q_in.1, bf16[256,768]{1,0:T(8,128)(2,1)} %kn_in.1, bf16[256,768]{1,0:T(8,128)(2,1)} %vn_in.1, bf16[16,16,768]{2,1,0:T(8,128)(2,1)} %bitcast.6, bf16[16,16,768]{2,1,0:T(8,128)(2,1)} %bitcast.7, bf16[4,48,768]{2,1,0:T(8,128)(2,1)} %bitcast.8, s32[32,62]{1,0:T(8,128)} %lists.1, ...), custom_call_target="tpu_custom_call" | custom-call | tf_op jit(solution)/shard_map/layer/pallas_call | solution.py:429
  97.3 1.8 %copy.11 = bf16[256,768]{1,0:T(8,128)(2,1)} copy(bf16[256,768]{1,0:T(8,128)(2,1)} %layer.1) | data formatting | bytes 786432
